TPU v7x, 32 devices: a whole 2x2x4 slice. The times are simulated.
32 devices in a mesh: dp: 8 (over y, x, core), seq: 4 (over z).
Axes of the slice: x: 2, y: 2, z: 4, core: 2. Of those that a mesh axis runs over, the one named last changes fastest.
Arguments:
- tokens: bfloat16 [32768, 768], P(('dp', 'seq')), may hold values from -6 to 6
- item_types: int32 [8, 64], P('dp'), may hold values from 0 to 3, as said below
- first_gain: float32 [768], replicated, may hold values from 0.5 to 1.5
- first_shift: float32 [768], replicated, may hold values from -4 to 4
- qkv_weight: bfloat16 [768, 2304], replicated, may hold values from -0.21875 to 0.21875
- query_bias: float32 [768], replicated, may hold values from -6 to 6
- value_bias: float32 [768], replicated, may hold values from -6 to 6
- attn_weight: bfloat16 [768, 768], replicated, may hold values from -1.75 to 1.75
- attn_bias: float32 [768], replicated, may hold values from -3 to 3
- second_gain: float32 [3, 768], replicated, may hold values from 0.5 to 1.5
- second_shift: float32 [3, 768], replicated, may hold values from -4 to 4
- expert_up: bfloat16 [3, 768, 3072], replicated, may hold values from -0.21875 to 0.21875
- up_bias: float32 [3, 3072], replicated, may hold values from -1.5 to 1.5
- expert_down: bfloat16 [3, 3072, 768], replicated, may hold values from -0.15625 to 0.15625
- down_bias: float32 [3, 768], replicated, may hold values from -1.5 to 1.5
- cotangent: bfloat16 [32768, 768], P(('dp', 'seq')), may hold values from -6 to 6
Outputs:
- mixed: bfloat16 [32768, 768], P(('dp', 'seq'))
- grad_tokens: float32 [32768, 768], P(('dp', 'seq'))
- grad_first_gain: float32 [768], P(('dp', 'seq'))
- grad_first_shift: float32 [768], P(('dp', 'seq'))
- grad_qkv_weight: float32 [768, 2304], P(None, ('dp', 'seq'))
- grad_query_bias: float32 [768], P(('dp', 'seq'))
- grad_value_bias: float32 [768], P(('dp', 'seq'))
- grad_attn_weight: float32 [768, 768], P(None, ('dp', 'seq'))
- grad_attn_bias: float32 [768], P(('dp', 'seq'))
- grad_second_gain: float32 [3, 768], P(None, ('dp', 'seq'))
- grad_second_shift: float32 [3, 768], P(None, ('dp', 'seq'))
- grad_expert_up: float32 [3, 768, 3072], P(None, ('dp', 'seq'))
- grad_up_bias: float32 [3, 3072], replicated
- grad_expert_down: float32 [3, 3072, 768], P(None, None, ('dp', 'seq'))
- grad_down_bias: float32 [3, 768], P(None, ('dp', 'seq'))
Inputs may be any that keep to these rules, and one draw needn't show every extreme that they name: `item_types`: 0, 1, 2 are image, text and image-text items, 3 an empty slot; the slots of a packed sequence are filled from the first, its items take at most 4096 tokens and leave fewer than 261 unused.
All inputs are finite; a program needn't handle non-finite values.
Results may differ from a plain program's by a relative error of at most 0.0095.
The roundings to bfloat16 on the way count: a program that leaves them out, or rounds other values in their place, can miss the bound.
Values may be sent and summed in bfloat16 or wider, within the bound.
No kernel may reach another device: no remote copies, remote signals or barrier semaphores. Data moves between devices by JAX's collectives and lax.ppermute only.
A program may use at most 384 MiB of HBM per device.

v0:
```python
from functools import partial

import jax
import jax.numpy as jnp
from jax import lax
from jax.sharding import PartitionSpec as P

HD = 64
EXPERTS = 3
QBLK = 512
IMG_LEN = 197
TXT_LEN = 64


EPS = 1e-05
NEG = -1e30
HIGH = lax.Precision.HIGHEST


def normalize(v):
    mean = jnp.mean(v, axis=-1, keepdims=True)
    cent = v - mean
    var = jnp.mean(cent * cent, axis=-1, keepdims=True)
    inverse = lax.rsqrt(var + EPS)
    return (cent * inverse, inverse)


def norm_back(grad, normed, inverse):
    inner = jnp.mean(grad * normed, axis=-1, keepdims=True)
    return inverse * (grad - jnp.mean(grad, axis=-1, keepdims=True) - normed * inner)


def layout(types_row, positions):
    lengths = jnp.where(
        types_row == 0,
        IMG_LEN,
        jnp.where(types_row == 1, TXT_LEN, jnp.where(types_row == 2, IMG_LEN + TXT_LEN, 0)),
    ).astype(jnp.int32)
    ends = jnp.cumsum(lengths)
    segment = jnp.sum((positions[:, None] >= ends[None, :]).astype(jnp.int32), axis=1)
    item_hot = (
        segment[:, None] == jnp.arange(types_row.shape[0], dtype=jnp.int32)[None, :]
    ).astype(jnp.float32)
    type_hot = (types_row[:, None] == jnp.arange(EXPERTS, dtype=jnp.int32)[None, :]).astype(
        jnp.float32
    )
    modal = jnp.dot(item_hot, type_hot, precision=HIGH)
    return (segment, modal)


def outer_dot(left, right):
    return lax.dot_general(
        left, right, (((0,), (0,)), ((), ())), preferred_element_type=jnp.float32
    )


def back_dot(left, right):
    return lax.dot_general(
        left, right, (((1,), (1,)), ((), ())), preferred_element_type=jnp.float32
    )


def window(index, group):
    start = index * QBLK
    begin = jnp.clip(start - QBLK, 0, group - 3 * QBLK)
    return (start, begin)


def masked_scores(query, keys, segment, start, begin):
    rows = lax.dynamic_slice_in_dim(query, start, QBLK, 0)
    cols = lax.dynamic_slice_in_dim(keys, begin, 3 * QBLK, 0)
    seg_rows = lax.dynamic_slice_in_dim(segment, start, QBLK, 0)
    seg_cols = lax.dynamic_slice_in_dim(segment, begin, 3 * QBLK, 0)
    scores = jnp.einsum("qhd,khd->hqk", rows, cols, preferred_element_type=jnp.float32)
    mask = (seg_rows[:, None] == seg_cols[None, :])[None]
    return (jnp.where(mask, scores, NEG), rows, cols)


def per_device(
    tokens,
    item_types,
    first_gain,
    first_shift,
    qkv_weight,
    query_bias,
    value_bias,
    attn_weight,
    attn_bias,
    second_gain,
    second_shift,
    expert_up,
    up_bias,
    expert_down,
    down_bias,
    cotangent,
):
    tok = tokens.shape[0]
    width = tokens.shape[1]
    ways = lax.axis_size("seq")
    group = tok * ways
    head_width = width // ways
    heads_here = head_width // HD
    blocks = group // QBLK
    scale = HD ** (-0.5)
    types_row = item_types[0]
    local_pos = lax.axis_index("seq") * tok + jnp.arange(tok, dtype=jnp.int32)
    _, modal = layout(types_row, local_pos)
    seg_group, _ = layout(types_row, jnp.arange(group, dtype=jnp.int32))
    inputs = tokens.astype(jnp.float32)
    grad_out = cotangent.astype(jnp.float32)
    normed_one, inverse_one = normalize(inputs)
    hidden_one = (normed_one * first_gain + first_shift).astype(jnp.bfloat16)
    bias_full = jnp.concatenate([query_bias, jnp.zeros((width,), jnp.float32), value_bias])
    scale_vec = jnp.concatenate(
        [jnp.full((width,), scale, jnp.float32), jnp.ones((2 * width,), jnp.float32)]
    )
    projected = (
        jnp.dot(hidden_one, qkv_weight, preferred_element_type=jnp.float32) + bias_full
    ) * scale_vec
    qkv_local = projected.astype(jnp.bfloat16).reshape(tok, 3, width)
    heads = lax.all_to_all(qkv_local, "seq", split_axis=2, concat_axis=0, tiled=True)
    query = heads[:, 0].reshape(group, heads_here, HD)
    keys = heads[:, 1].reshape(group, heads_here, HD)
    values = heads[:, 2].reshape(group, heads_here, HD)

    def attend_block(index):
        start, begin = window(index, group)
        masked, rows, cols = masked_scores(query, keys, seg_group, start, begin)
        top = jnp.max(masked, axis=-1, keepdims=True)
        expo = jnp.exp(masked - top)
        total = jnp.sum(expo, axis=-1, keepdims=True)
        prob = (expo / total).astype(jnp.bfloat16)
        vals = lax.dynamic_slice_in_dim(values, begin, 3 * QBLK, 0)
        result = jnp.einsum("hqk,khd->qhd", prob, vals, preferred_element_type=jnp.float32)
        return (result, top, total)

    block_ids = jnp.arange(blocks, dtype=jnp.int32)
    attended_heads, tops, totals = lax.map(attend_block, block_ids)
    attended_heads = attended_heads.reshape(group, head_width).astype(jnp.bfloat16)
    attended = lax.all_to_all(attended_heads, "seq", split_axis=0, concat_axis=1, tiled=True)
    middle = inputs + jnp.dot(attended, attn_weight, preferred_element_type=jnp.float32) + attn_bias
    normed_two, inverse_two = normalize(middle)
    gains = jnp.dot(modal, second_gain, precision=HIGH)
    shifts = jnp.dot(modal, second_shift, precision=HIGH)
    hidden_two = (normed_two * gains + shifts).astype(jnp.bfloat16)
    branch = jnp.zeros_like(middle)
    kept_active = []
    kept_back = []
    for expert in range(EXPERTS):
        upper = (
            jnp.dot(hidden_two, expert_up[expert], preferred_element_type=jnp.float32)
            + up_bias[expert]
        )
        active, gelu_back = jax.vjp(partial(jax.nn.gelu, approximate=False), upper)
        active_low = active.astype(jnp.bfloat16)
        lower = (
            jnp.dot(active_low, expert_down[expert], preferred_element_type=jnp.float32)
            + down_bias[expert]
        )
        branch = branch + modal[:, expert : expert + 1] * lower
        kept_active.append(active_low)
        kept_back.append(gelu_back)
    mixed = (middle + branch).astype(jnp.bfloat16)
    grad_hidden_two = jnp.zeros_like(middle)
    grad_up_list = []
    grad_up_bias_list = []
    grad_down_list = []
    grad_down_bias_list = []
    for expert in range(EXPERTS):
        selected = modal[:, expert : expert + 1] * grad_out
        selected_low = selected.astype(jnp.bfloat16)
        grad_down_bias_list.append(jnp.sum(selected, axis=0))
        grad_down_list.append(outer_dot(kept_active[expert], selected_low))
        grad_active = back_dot(selected_low, expert_down[expert])
        grad_upper = kept_back[expert](grad_active)[0].astype(jnp.bfloat16)
        grad_up_bias_list.append(jnp.sum(grad_upper.astype(jnp.float32), axis=0))
        grad_up_list.append(outer_dot(hidden_two, grad_upper))
        grad_hidden_two = grad_hidden_two + back_dot(grad_upper, expert_up[expert])
    grad_up = jnp.stack(grad_up_list)
    grad_up_bias = jnp.stack(grad_up_bias_list)
    grad_down = jnp.stack(grad_down_list)
    grad_down_bias = jnp.stack(grad_down_bias_list)
    sum_up_bias = lax.psum(grad_up_bias, ("dp", "seq"))
    grad_second_gain = lax.dot_general(
        modal, grad_hidden_two * normed_two, (((0,), (0,)), ((), ())), precision=HIGH
    )
    grad_second_shift = lax.dot_general(
        modal, grad_hidden_two, (((0,), (0,)), ((), ())), precision=HIGH
    )
    grad_middle = grad_out + norm_back(grad_hidden_two * gains, normed_two, inverse_two)
    grad_proj = grad_middle.astype(jnp.bfloat16)
    grad_attn_bias = jnp.sum(grad_proj.astype(jnp.float32), axis=0)
    grad_attn_weight = outer_dot(attended, grad_proj)
    grad_attended = back_dot(grad_proj, attn_weight).astype(jnp.bfloat16)
    grad_heads = lax.all_to_all(
        grad_attended, "seq", split_axis=1, concat_axis=0, tiled=True
    ).reshape(group, heads_here, HD)

    def grad_block(carry, inputs_block):
        grad_keys, grad_values = carry
        index, top, total = inputs_block
        start, begin = window(index, group)
        masked, rows, cols = masked_scores(query, keys, seg_group, start, begin)
        prob = jnp.exp(masked - top) / total
        prob_low = prob.astype(jnp.bfloat16)
        vals = lax.dynamic_slice_in_dim(values, begin, 3 * QBLK, 0)
        grad_rows = lax.dynamic_slice_in_dim(grad_heads, start, QBLK, 0)
        grad_prob = jnp.einsum("qhd,khd->hqk", grad_rows, vals, preferred_element_type=jnp.float32)
        row_inner = jnp.sum(prob * grad_prob, axis=-1, keepdims=True)
        grad_score = (prob * (grad_prob - row_inner)).astype(jnp.bfloat16)
        grad_query = jnp.einsum(
            "hqk,khd->qhd", grad_score, cols, preferred_element_type=jnp.float32
        )
        grad_key = jnp.einsum("hqk,qhd->khd", grad_score, rows, preferred_element_type=jnp.float32)
        grad_value = jnp.einsum(
            "hqk,qhd->khd", prob_low, grad_rows, preferred_element_type=jnp.float32
        )
        grad_keys = lax.dynamic_update_slice_in_dim(
            grad_keys, lax.dynamic_slice_in_dim(grad_keys, begin, 3 * QBLK, 0) + grad_key, begin, 0
        )
        grad_values = lax.dynamic_update_slice_in_dim(
            grad_values,
            lax.dynamic_slice_in_dim(grad_values, begin, 3 * QBLK, 0) + grad_value,
            begin,
            0,
        )
        return ((grad_keys, grad_values), grad_query)

    start_carry = (
        jnp.zeros((group, heads_here, HD), jnp.float32),
        jnp.zeros((group, heads_here, HD), jnp.float32),
    )
    (grad_keys, grad_values), grad_queries = lax.scan(
        grad_block, start_carry, (block_ids, tops, totals)
    )
    grad_stack = jnp.stack(
        [
            grad_queries.reshape(group, head_width),
            grad_keys.reshape(group, head_width),
            grad_values.reshape(group, head_width),
        ],
        axis=1,
    ).astype(jnp.bfloat16)
    grad_local = lax.all_to_all(grad_stack, "seq", split_axis=0, concat_axis=2, tiled=True).reshape(
        tok, 3 * width
    )
    grad_pre = grad_local.astype(jnp.float32) * scale_vec
    grad_pre_low = grad_pre.astype(jnp.bfloat16)
    grad_qkv = outer_dot(hidden_one, grad_pre_low)
    grad_query_bias = jnp.sum(grad_pre[:, :width], axis=0)
    grad_value_bias = jnp.sum(grad_pre[:, 2 * width :], axis=0)
    grad_hidden_one = back_dot(grad_pre_low, qkv_weight)
    grad_first_gain = jnp.sum(grad_hidden_one * normed_one, axis=0)
    grad_first_shift = jnp.sum(grad_hidden_one, axis=0)
    grad_inputs = grad_middle + norm_back(grad_hidden_one * first_gain, normed_one, inverse_one)
    summed = (
        lax.psum_scatter(grad_first_gain, ("dp", "seq"), scatter_dimension=0, tiled=True),
        lax.psum_scatter(grad_first_shift, ("dp", "seq"), scatter_dimension=0, tiled=True),
        lax.psum_scatter(grad_qkv, ("dp", "seq"), scatter_dimension=1, tiled=True),
        lax.psum_scatter(grad_query_bias, ("dp", "seq"), scatter_dimension=0, tiled=True),
        lax.psum_scatter(grad_value_bias, ("dp", "seq"), scatter_dimension=0, tiled=True),
        lax.psum_scatter(grad_attn_weight, ("dp", "seq"), scatter_dimension=1, tiled=True),
        lax.psum_scatter(grad_attn_bias, ("dp", "seq"), scatter_dimension=0, tiled=True),
        lax.psum_scatter(grad_second_gain, ("dp", "seq"), scatter_dimension=1, tiled=True),
        lax.psum_scatter(grad_second_shift, ("dp", "seq"), scatter_dimension=1, tiled=True),
        lax.psum_scatter(grad_up, ("dp", "seq"), scatter_dimension=1, tiled=True),
        lax.psum_scatter(grad_down, ("dp", "seq"), scatter_dimension=2, tiled=True),
        lax.psum_scatter(grad_down_bias, ("dp", "seq"), scatter_dimension=1, tiled=True),
    )
    (
        sum_first_gain,
        sum_first_shift,
        sum_qkv,
        sum_query,
        sum_value,
        sum_attn,
        sum_attn_bias,
        sum_second_gain,
        sum_second_shift,
        sum_up,
        sum_down,
        sum_down_bias,
    ) = summed
    return (
        mixed,
        grad_inputs,
        sum_first_gain,
        sum_first_shift,
        sum_qkv,
        sum_query,
        sum_value,
        sum_attn,
        sum_attn_bias,
        sum_second_gain,
        sum_second_shift,
        sum_up,
        sum_up_bias,
        sum_down,
        sum_down_bias,
    )


def solution(mesh):
    in_specs = (
        P(("dp", "seq"), None),
        P("dp", None),
        P(),
        P(),
        P(),
        P(),
        P(),
        P(),
        P(),
        P(),
        P(),
        P(),
        P(),
        P(),
        P(),
        P(("dp", "seq"), None),
    )
    out_specs = (
        P(("dp", "seq"), None),
        P(("dp", "seq"), None),
        P(("dp", "seq")),
        P(("dp", "seq")),
        P(None, ("dp", "seq")),
        P(("dp", "seq")),
        P(("dp", "seq")),
        P(None, ("dp", "seq")),
        P(("dp", "seq")),
        P(None, ("dp", "seq")),
        P(None, ("dp", "seq")),
        P(None, ("dp", "seq"), None),
        P(),
        P(None, None, ("dp", "seq")),
        P(None, ("dp", "seq")),
    )
    return jax.shard_map(
        per_device, mesh=mesh, in_specs=in_specs, out_specs=out_specs, check_vma=False
    )
```

profile of v0, /device:TPU:0, one launch (start us, length us, event | category | flops | bytes accessed | tf_op | source)
XLA Modules:
  0.0 2515.5 jit_solution(1568229604140704358)
XLA Ops:
  29.0 9.1 copy.136
  49.0 134.3 %all-to-all-done = bf16[1024,3,768]{0,1,2:T(4,128)(2,1)} async-done(((bf16[1024,3,768]{0,1,2:T(4,128)(2,1)}), bf16[1024,3,768]{0,1,2:T(4,128)(2,1)}, u32[]{:S(2)}, u32[]{:S(2)}) %all-to-all-start) | async-done | bytes 4718624 | tf_op jit(solution)/shard_map/all_to_all | solution.py:121
  192.8 109.8 %while.32 = (s32[]{:T(128)}, bf16[8,512,3,64]{1,3,2,0:T(8,128)(2,1)}, f32[8,3,512,1]{2,1,3,0:T(4,128)}, f32[8,3,512,1]{2,1,3,0:T(4,128)}, s32[8]{0:T(128)}, /*in...) while((s32[]{:T(128)}, ...), condition=%wide.region_7.8_spmd, body=%wide.region_4.7_spmd.sunk | while | flops 625996800 | bytes 33310992 | solution.py:138
  329.2 25.1 all-to-all-done.1
  362.0 36.9 %multiply_convert_fusion.1 = (bf16[1024,3072]{1,0:T(8,128)(2,1)}, f32[1024,3072]{1,0:T(8,128)}, f32[1024,3072]{1,0:T(8,128)}) fusion(f32[3072]{0:T(1024)S(1)} %bitcast.218, bf16[1024,768]{0,1:T(8,128)(2,1)S(1)} %add_convert_fusion.4, bf16[3,768,3072]{2,1,0:T(8,128)(2,1)} %param.31), kind=kOutput, calls=%fused_computation.58 | convolution fusion | flops 5039456256 | bytes 37761024 | tf_op jit(solution)/shard_map/dot_general | solution.py:151
  399.0 17.7 convert_reduce_fusion
  416.7 9.9 fusion.55
  426.7 33.6 %multiply_convert_fusion.2 = (bf16[1024,3072]{1,0:T(8,128)(2,1)}, f32[1024,3072]{1,0:T(8,128)}, f32[1024,3072]{1,0:T(8,128)}) fusion(f32[3072]{0:T(1024)S(1)} %bitcast.216, bf16[1024,768]{0,1:T(8,128)(2,1)S(1)} %add_convert_fusion.4, bf16[3,768,3072]{2,1,0:T(8,128)(2,1)S(1)} %copy-done.47), kind=kOutput, calls=%fused_computation.71 | convolution fusion | flops 5039456256 | bytes 37761024 | tf_op jit(solution)/shard_map/dot_general | solution.py:151
  460.3 17.9 convert_reduce_fusion.1
  478.2 9.9 fusion.62
  488.1 33.6 %multiply_convert_fusion.3 = (bf16[1024,3072]{1,0:T(8,128)(2,1)}, f32[1024,3072]{1,0:T(8,128)}, f32[1024,3072]{1,0:T(8,128)}) fusion(f32[3072]{0:T(1024)S(1)} %bitcast.214, bf16[1024,768]{0,1:T(8,128)(2,1)S(1)} %add_convert_fusion.4, bf16[3,768,3072]{2,1,0:T(8,128)(2,1)S(1)} %copy-done.48), kind=kOutput, calls=%fused_computation.84 | convolution fusion | flops 5039456256 | bytes 37761024 | tf_op jit(solution)/shard_map/dot_general | solution.py:151
  521.8 19.6 convert_reduce_fusion.2
  541.4 12.4 fusion.133
  565.3 36.5 %all-to-all-done.2 = bf16[1024,4,192]{0,2,1:T(8,128)(2,1)} async-done(((bf16[1024,4,192]{0,2,1:T(8,128)(2,1)}), bf16[1024,4,192]{0,2,1:T(8,128)(2,1)}, u32[]{:S(2)}, u32[]{:S(2)}) %all-to-all-start.2) | async-done | bytes 1572896 | tf_op jit(solution)/shard_map/all_to_all | solution.py:195
  615.4 421.8 %while.33 = (s32[]{:T(128)}, f32[4096,3,64]{0,2,1:T(8,128)}, f32[4096,3,64]{0,2,1:T(8,128)}, bf16[8,512,3,64]{1,3,2,0:T(8,128)(2,1)}, s32[8]{0:T(128)}, /*index=...) while((s32[]{:T(128)}, f32[4096,3,64]{0,2,1:T(8,128)}, ...), condition=%wide.region_15.16_spmd, body=%wide.region_13.15_spmd.sunk | while | flops 1532557824 | bytes 141435264 | solution.py:233
  621.4 8.7 multiply_reduce_fusion.5
  630.1 9.4 multiply_convert_fusion.6
  674.6 8.7 multiply_reduce_fusion.5
  683.3 9.4 multiply_convert_fusion.6
  727.9 8.7 multiply_reduce_fusion.5
  736.6 9.4 multiply_convert_fusion.6
  781.2 8.7 multiply_reduce_fusion.5
  789.9 9.4 multiply_convert_fusion.6
  834.5 8.7 multiply_reduce_fusion.5
  843.2 9.4 multiply_convert_fusion.6
  887.4 8.7 multiply_reduce_fusion.5
  896.1 9.4 multiply_convert_fusion.6
  948.7 9.4 multiply_convert_fusion.6
  1000.2 9.4 multiply_convert_fusion.6
  1051.1 12.7 copy.149
  1085.8 10.5 convolution_bitcast_fusion.2
  1111.8 140.5 %all-to-all-done.3 = bf16[4096,3,192]{2,1,0:T(4,128)(2,1)} async-done(((bf16[4096,3,192]{2,1,0:T(4,128)(2,1)}), bf16[4096,3,192]{2,1,0:T(4,128)(2,1)}, u32[]{:S(2)}, u32[]{:S(2)}) %all-to-all-start.3) | async-done | bytes 4718624 | tf_op jit(solution)/shard_map/all_to_all | solution.py:244
  1252.3 12.8 copy.150
  1265.0 12.1 reshape.207
  1277.2 12.8 copy.151
  1289.9 9.6 copy.152
  1299.5 9.9 fusion.141
  1325.1 21.2 pad_maximum_fusion.1
  1346.3 40.4 %copy.155 = f32[3,3072,768]{1,0,2:T(4,128)} copy(f32[3,3072,768]{2,1,0:T(8,128)} %pad_maximum_fusion.1) | data formatting | bytes 56623104 | tf_op jit(solution)/shard_map/stack | solution.py:181
  1392.1 11.3 fusion.108
  1425.5 10.0 pad_maximum_fusion
  1436.4 10.0 fusion.53
  1446.3 9.9 fusion.60
  1456.3 10.6 add_convert_fusion.3
  1490.2 517.6 %all-reduce.13.cloned.1.call-done = f32[3,3072,768]{1,0,2:T(4,128)} async-done(((f32[3,3072,768]{1,0,2:T(4,128)}), f32[3,3072,768]{1,0,2:T(4,128)}) %all-reduce.13.cloned.1.call-update) | async-done | bytes 28311568
  2010.6 102.8 %reduce-scatter.9.cloned.1.call-done = f32[768,24]{0,1:T(8,128)} async-done(((f32[768,768]{0,1:T(8,128)}), f32[768,24]{0,1:T(8,128)}) %reduce-scatter.9.cloned.1.call-update) | async-done | bytes 73744 | tf_op jit(solution)/shard_map/reduce_scatter | solution.py:262
  2113.4 124.4 %reduce-scatter.7.cloned.1.call-done = f32[768,72]{0,1:T(8,128)} async-done(((f32[768,2304]{0,1:T(8,128)}), f32[768,72]{0,1:T(8,128)}) %reduce-scatter.7.cloned.1.call-update) | async-done | bytes 221200 | tf_op jit(solution)/shard_map/reduce_scatter | solution.py:259
  2237.8 269.3 %reduce-scatter.11.cloned.1.call-done = f32[3,24,3072]{2,1,0:T(8,128)} async-done(((f32[3,768,3072]{2,1,0:T(8,128)}), f32[3,24,3072]{2,1,0:T(8,128)}) %reduce-scatter.11.cloned.1.call-update) | async-done | bytes 884752 | tf_op jit(solution)/shard_map/reduce_scatter | solution.py:266
  (398 shorter events, 617.6 us)
Async XLA Ops:
  29.0 15.6 copy-start.50
  38.0 145.3 %all-to-all-start = ((bf16[1024,3,768]{0,1,2:T(4,128)(2,1)}), bf16[1024,3,768]{0,1,2:T(4,128)(2,1)}, u32[]{:S(2)}, u32[]{:S(2)}) async-start(bf16[1024,3,768]{0,1,2:T(4,128)(2,1)} %copy.136), calls=%async_computation | async-start | bytes 12582912 | tf_op jit(solution)/shard_map/all_to_all | solution.py:121
  302.6 25.0 copy-start.15
  312.8 41.5 %all-to-all-start.1 = ((bf16[4,1024,192]{1,2,0:T(8,128)(2,1)}), bf16[4,1024,192]{1,2,0:T(8,128)(2,1)}, u32[]{:S(2)}, u32[]{:S(2)}) async-start(bf16[4,1024,192]{1,2,0:T(8,128)(2,1)} %copy.141), calls=%async_computation.1 | async-start | bytes 3145728 | tf_op jit(solution)/shard_map/all_to_all | solution.py:140
  329.2 29.6 %copy-start.18 = (f32[1024,3]{0,1:T(4,128)S(1)}, f32[1024,3]{0,1:T(4,128)}, u32[]{:S(2)}) copy-start(f32[1024,3]{0,1:T(4,128)} %copy-done.17) | copy-start | bytes 36868
  358.4 40.6 %copy-start.3 = (f32[1024,768]{0,1:T(8,128)}, f32[1024,768]{0,1:T(8,128)S(1)}, u32[]{:S(2)}) copy-start(f32[1024,768]{0,1:T(8,128)S(1)} %get-tuple-element.470) | copy-start | bytes 9437188
  358.4 40.6 %copy-start.20 = (f32[1024]{0:T(1024)}, f32[1024]{0:T(1024)S(1)}, u32[]{:S(2)}) copy-start(f32[1024]{0:T(1024)S(1)} %broadcast_multiply_fusion.5) | copy-start | bytes 12292
  358.8 40.2 %copy-start.24 = (f32[1024]{0:T(1024)}, f32[1024]{0:T(1024)S(1)}, u32[]{:S(2)}) copy-start(f32[1024]{0:T(1024)S(1)} %add_rsqrt_fusion) | copy-start | bytes 12292
  362.0 126.1 %copy-start.13 = (bf16[1024,768]{0,1:T(8,128)(2,1)}, bf16[1024,768]{0,1:T(8,128)(2,1)S(1)}, u32[]{:S(2)}) copy-start(bf16[1024,768]{0,1:T(8,128)(2,1)S(1)} %add_convert_fusion.4) | copy-start | bytes 4718596
  362.0 37.0 %copy-start.10 = (bf16[1024,768]{0,1:T(8,128)(2,1)S(1)}, bf16[1024,768]{0,1:T(8,128)(2,1)}, u32[]{:S(2)}) copy-start(bf16[1024,768]{0,1:T(8,128)(2,1)} %copy.146) | copy-start | bytes 4718596
  362.0 37.0 %copy-start.32 = (f32[1024,1]{0,1:T(1,128)S(1)}, f32[1024,1]{0,1:T(1,128)}, u32[]{:S(2)}) copy-start(f32[1024,1]{0,1:T(1,128)} %get-tuple-element.467) | copy-start | bytes 12292
  362.0 37.0 %copy-start.46 = (f32[1,3072]{1,0:T(1,128)S(1)}, f32[1,3072]{1,0:T(1,128)}, u32[]{:S(2)}) copy-start(f32[1,3072]{1,0:T(1,128)} %get-tuple-element.464) | copy-start | bytes 36868
  416.7 10.0 copy-start.44
  416.7 10.0 copy-start.47
  426.7 33.6 %copy-start.36 = (f32[1024,1]{0,1:T(1,128)S(1)}, f32[1024,1]{0,1:T(1,128)}, u32[]{:S(2)}) copy-start(f32[1024,1]{0,1:T(1,128)} %get-tuple-element.468) | copy-start | bytes 12292
  478.2 9.9 copy-start.43
  478.2 9.9 copy-start.48
  488.1 33.6 %copy-start.29 = (f32[1024,1]{0,1:T(1,128)S(1)}, f32[1024,1]{0,1:T(1,128)}, u32[]{:S(2)}) copy-start(f32[1024,1]{0,1:T(1,128)} %get-tuple-element.466) | copy-start | bytes 12292
  521.7 19.6 copy-start.4
  521.8 19.6 copy-start.21
  521.8 19.6 copy-start.25
  541.4 12.4 copy-start.11
  541.4 12.4 copy-start.33
  541.4 12.4 copy-start.37
  560.7 54.7 %copy-start.16 = (s32[4096]{0:T(1024)S(1)}, s32[4096]{0:T(1024)}, u32[]{:S(2)}) copy-start(s32[4096]{0:T(1024)} %copy-done.15) | copy-start | bytes 49156
  560.7 41.2 %all-to-all-start.2 = ((bf16[1024,4,192]{0,2,1:T(8,128)(2,1)}), bf16[1024,4,192]{0,2,1:T(8,128)(2,1)}, u32[]{:S(2)}, u32[]{:S(2)}) async-start(bf16[1024,4,192]{0,2,1:T(8,128)(2,1)} %bitcast.201), calls=%async_computation.2 | async-start | bytes 3145728 | tf_op jit(solution)/shard_map/all_to_all | solution.py:195
  1063.8 9.1 copy-start.19
  1063.8 188.4 %all-to-all-start.3 = ((bf16[4096,3,192]{2,1,0:T(4,128)(2,1)}), bf16[4096,3,192]{2,1,0:T(4,128)(2,1)}, u32[]{:S(2)}, u32[]{:S(2)}) async-start(bf16[4096,3,192]{2,1,0:T(4,128)(2,1)} %copy.149), calls=%async_computation.3 | async-start | bytes 16777216 | tf_op jit(solution)/shard_map/all_to_all | solution.py:244
  1069.7 410.2 %all-reduce.15.cloned.1.call-start = ((), (), s32[]{:S(2)}) async-start(), calls=%async_computation.11 | async-start | bytes 212992
  1070.2 15.6 copy-start.12
  1070.2 15.6 copy-start.34
  1079.5 16.8 slice-start
  1085.8 10.5 copy-start.38
  1085.8 10.5 slice-start.1
  1085.8 18.2 slice-start.2
  1289.9 9.6 copy-start.41
  1299.5 9.9 copy-start.6
  1299.5 9.9 copy-start.42
  1325.1 682.6 %all-reduce.13.cloned.1.call-start = ((), (), s32[]{:S(2)}) async-start(), calls=%async_computation.10 | async-start | bytes 75497472
  1386.8 726.7 %reduce-scatter.9.cloned.1.call-start = ((), (), s32[]{:S(2)}) async-start(), calls=%async_computation.8 | async-start | bytes 2433024 | tf_op jit(solution)/shard_map/reduce_scatter | solution.py:262
  1392.0 845.8 %reduce-scatter.7.cloned.1.call-start = ((), (), s32[]{:S(2)}) async-start(), calls=%async_computation.7 | async-start | bytes 7299072 | tf_op jit(solution)/shard_map/reduce_scatter | solution.py:259
  1403.5 1103.7 %reduce-scatter.11.cloned.1.call-start = ((), (), s32[]{:S(2)}) async-start(), calls=%async_computation.9 | async-start | bytes 29196288 | tf_op jit(solution)/shard_map/reduce_scatter | solution.py:266
  1436.3 19.9 slice-start.4
  1446.3 9.9 copy-start.5
  1446.3 9.9 copy-start.31
  1446.3 10.0 copy-start.35
  1446.3 10.0 copy-start.39
  1446.3 10.0 slice-start.5
  (32 other events, 203.7 us)
Sparse Core Ops, SparseCore 0:
  1325.2 124.1 all-reduce.14
  1457.0 550.6 all-reduce.12
  2014.4 98.9 reduce-scatter.8
  2119.5 118.2 reduce-scatter.6
  2245.8 261.2 reduce-scatter.10
where the time goes:
time: 2530 us; the launch traced here: 2520 us
  waiting for transfers between devices  1350 us (53%)
  matrix products  589 us (23%)
  local copies, waits for them, and re-layouts  353 us (14%)
  other arithmetic  174 us (7%)
    unnamed x7, waiting for transfers between devices  518 us
    reduce_scatter x1, waiting for transfers between devices, per_device(): lax.psum_scatter(grad_up, ('dp', 'seq'), scatter_dimension=1, tiled=True)  269 us
    all_to_all x1, waiting for transfers between devices, per_device(): lax.all_to_all(grad_stack, 'seq', split_axis=0, concat_axis=2, tiled=True)  141 us
    all_to_all x1, waiting for transfers between devices, per_device(): lax.all_to_all(qkv_local, 'seq', split_axis=2, concat_axis=0, tiled=True)  134 us
    reduce_scatter x1, waiting for transfers between devices, per_device(): lax.psum_scatter(grad_qkv, ('dp', 'seq'), scatter_dimension=1, tiled=True)  124 us
    dot_general x3, matrix products, per_device(): jnp.dot(hidden_two, expert_up[expert], preferred_element_type=jnp.float32)  104 us
    reduce_scatter x1, waiting for transfers between devices, per_device(): lax.psum_scatter(grad_attn_weight, ('dp', 'seq'), scatter_dimension=1, ti...  103 us
    dot_general x8, matrix products, back_dot(): lax.dot_general(left, right, (((1,), (1,)), ((), ())), preferred_element_...  100 us
  transfers between devices with their start and end apart: 9, of which 8 were waited for; matrix products, arithmetic and copies ran while one was open for 9% of the time, Pallas kernels for 0%

commit v1 on v0

v1 whole, which is shorter than its diff:
```python
from functools import partial

import jax
import jax.numpy as jnp
from jax import lax
from jax.experimental import pallas as pl
from jax.experimental.pallas import tpu as pltpu
from jax.sharding import PartitionSpec as P

HD = 64
EXPERTS = 3
IMG_LEN = 197
TXT_LEN = 64
LENS = (IMG_LEN, TXT_LEN, IMG_LEN + TXT_LEN)
SLOTS = (208, 64, 272)
TXT_PAIR = 128
PAD_ROWS = 384
HALO = 144
ROW = 128
BLK = 256

EPS = 1e-05
NEG = -1e30
VMEM = 60 << 20
F32 = jnp.float32
BF16 = jnp.bfloat16

N_IMG, N_TXT, N_BOTH, N_PAD = 0, 1, 2, 3
G_IMG, G_TXT, G_BOTH, G_PAD, G_END = 4, 5, 6, 7, 8
PAD_LEN, OWN_N = 9, 10
TABLE = 16
INFO = 256


def nn(a, b):
    return lax.dot_general(a, b, (((1,), (0,)), ((), ())), preferred_element_type=F32)


def nt(a, b):
    return lax.dot_general(a, b, (((1,), (1,)), ((), ())), preferred_element_type=F32)


def tn(a, b):
    return lax.dot_general(a, b, (((0,), (0,)), ((), ())), preferred_element_type=F32)


def up_to(value, unit):
    return ((value + unit - 1) // unit) * unit


def normalize(v):
    mean = jnp.mean(v, axis=-1, keepdims=True)
    cent = v - mean
    var = jnp.mean(cent * cent, axis=-1, keepdims=True)
    inverse = lax.rsqrt(var + EPS)
    return (cent * inverse, inverse)


def norm_back(grad, normed, inverse):
    inner = jnp.mean(grad * normed, axis=-1, keepdims=True)
    return inverse * (grad - jnp.mean(grad, axis=-1, keepdims=True) - normed * inner)


def capacity(tok):
    rows = tok + LENS[2] - 1
    best = 0
    for images in range(rows // LENS[0] + 1):
        for both in range((rows - images * LENS[0]) // LENS[2] + 1):
            left = rows - images * LENS[0] - both * LENS[2]
            for pad in (0, 1):
                spare = left - pad * (1 + LENS[2] // 2)
                if spare < 0:
                    continue
                texts = spare // LENS[1]
                for count in range(texts + 1):
                    total = (
                        up_to(images * SLOTS[0], ROW)
                        + up_to(count * SLOTS[1], ROW)
                        + up_to(both * SLOTS[2], ROW)
                        + pad * PAD_ROWS
                    )
                    best = max(best, total)
    return up_to(best, BLK)


def sort_kernel(
    tok, group, pos, types, x_left, x_own, x_right, d_left, d_own, d_right,
    x_out, d_out, info, x_win, d_win,
):
    items = types.shape[1]
    low = pos[0] * tok
    for win, parts in ((x_win, (x_left, x_own, x_right)), (d_win, (d_left, d_own, d_right))):
        win[pl.ds(0, HALO), :] = parts[0][...]
        win[pl.ds(HALO, tok), :] = parts[1][...]
        win[pl.ds(HALO + tok, HALO), :] = parts[2][...]
        rest = win.shape[0] - (2 * HALO + tok)
        win[pl.ds(2 * HALO + tok, rest), :] = jnp.zeros((rest, win.shape[1]), win.dtype)

    def length(kind):
        return jnp.where(
            kind == 0, LENS[0], jnp.where(kind == 1, LENS[1], jnp.where(kind == 2, LENS[2], 0))
        )

    def owned(start, size):
        middle = (start + start + size) // 2
        return (middle >= low) & (middle < low + tok) & (size > 0)

    def count(index, carry):
        start, images, texts, boths = carry
        kind = types[0, index]
        size = length(kind)
        mine = owned(start, size)
        return (
            start + size,
            images + jnp.where(mine & (kind == 0), 1, 0),
            texts + jnp.where(mine & (kind == 1), 1, 0),
            boths + jnp.where(mine & (kind == 2), 1, 0),
        )

    zero = jnp.int32(0)
    total, images, texts, boths = lax.fori_loop(0, items, count, (zero, zero, zero, zero))
    pad_len = group - total
    pad = owned(total, pad_len)
    g_txt = up_to(images * SLOTS[0], ROW)
    g_both = g_txt + up_to(texts * SLOTS[1], ROW)
    g_pad = g_both + up_to(boths * SLOTS[2], ROW)
    g_end = g_pad + jnp.where(pad, PAD_ROWS, 0)
    info[N_IMG] = images
    info[N_TXT] = texts
    info[N_BOTH] = boths
    info[N_PAD] = jnp.where(pad, 1, 0)
    info[G_IMG] = zero
    info[G_TXT] = g_txt
    info[G_BOTH] = g_both
    info[G_PAD] = g_pad
    info[G_END] = g_end
    info[PAD_LEN] = pad_len
    x_out[...] = jnp.zeros_like(x_out)
    d_out[...] = jnp.zeros_like(d_out)

    def copy_rows(source, target, size, slot):
        begin = pl.multiple_of((source // 16) * 16, 16)
        shift = source - begin
        rows = lax.broadcasted_iota(jnp.int32, (slot, slot + 16), 0)
        cols = lax.broadcasted_iota(jnp.int32, (slot, slot + 16), 1)
        chosen = ((cols == rows + shift) & (rows < size)).astype(F32).astype(BF16)
        for win, out in ((x_win, x_out), (d_win, d_out)):
            out[pl.ds(target, slot), :] = nn(chosen, win[pl.ds(begin, slot + 16), :]).astype(BF16)

    def place(index, carry):
        start, images, texts, boths, own = carry
        kind = types[0, index]
        size = length(kind)
        mine = owned(start, size)
        source = start - low + HALO
        target = jnp.where(
            kind == 0,
            images * SLOTS[0],
            jnp.where(kind == 1, g_txt + texts * SLOTS[1], g_both + boths * SLOTS[2]),
        )
        target = pl.multiple_of(target, 16)

        @pl.when(mine)
        def _():
            info[TABLE + 3 * own] = source
            info[TABLE + 3 * own + 1] = target
            info[TABLE + 3 * own + 2] = kind

        for which in range(EXPERTS):

            @pl.when(mine & (kind == which))
            def _(which=which):
                copy_rows(source, target, LENS[which], SLOTS[which])

        return (
            start + size,
            images + jnp.where(mine & (kind == 0), 1, 0),
            texts + jnp.where(mine & (kind == 1), 1, 0),
            boths + jnp.where(mine & (kind == 2), 1, 0),
            own + jnp.where(mine, 1, 0),
        )

    own = lax.fori_loop(0, items, place, (zero, zero, zero, zero, zero))[-1]
    pad_source = total - low + HALO

    @pl.when(pad)
    def _():
        copy_rows(pad_source, pl.multiple_of(g_pad, ROW), pad_len, SLOTS[2])
        info[TABLE + 3 * own] = pad_source
        info[TABLE + 3 * own + 1] = g_pad
        info[TABLE + 3 * own + 2] = 3

    info[OWN_N] = own + jnp.where(pad, 1, 0)


def sort_rows(seq, types, x_parts, d_parts, rows, tok, group):
    width = x_parts[1].shape[1]
    smem = pl.BlockSpec(memory_space=pltpu.SMEM)
    vmem = pl.BlockSpec(memory_space=pltpu.VMEM)
    spare = tok + HALO + 288
    return pl.pallas_call(
        partial(sort_kernel, tok, group),
        out_shape=[
            jax.ShapeDtypeStruct((rows, width), BF16),
            jax.ShapeDtypeStruct((rows, width), BF16),
            jax.ShapeDtypeStruct((INFO,), jnp.int32),
        ],
        in_specs=[smem, smem] + [vmem] * 6,
        out_specs=[vmem, vmem, smem],
        scratch_shapes=[pltpu.VMEM((spare, width), BF16)] * 2,
        compiler_params=pltpu.CompilerParams(vmem_limit_bytes=VMEM),
        name="sort_rows",
    )(seq, types, *x_parts, *d_parts)


def unsort_kernel(tok, info, mixed, grad, m_own, m_left, m_right, g_own, g_left, g_right, m_win, g_win):
    m_win[...] = jnp.zeros_like(m_win)
    g_win[...] = jnp.zeros_like(g_win)

    def place(index, carry):
        source = info[TABLE + 3 * index]
        target = pl.multiple_of(info[TABLE + 3 * index + 1], 16)
        kind = info[TABLE + 3 * index + 2]
        begin = pl.multiple_of((source // 16) * 16, 16)
        shift = source - begin
        for which in range(EXPERTS):
            slot = SLOTS[which]
            fits = (kind == which) if which < 2 else (kind >= 2)
            size = LENS[which] if which < 2 else jnp.where(kind == 2, LENS[2], info[PAD_LEN])

            @pl.when(fits)
            def _(slot=slot, size=size):
                rows = lax.broadcasted_iota(jnp.int32, (slot + 16, slot), 0)
                cols = lax.broadcasted_iota(jnp.int32, (slot + 16, slot), 1)
                chosen = ((rows == cols + shift) & (cols < size)).astype(F32).astype(BF16)
                at, to = pl.ds(target, slot), pl.ds(begin, slot + 16)
                m_win[to, :] += nn(chosen, mixed[at, :])
                value = grad[at, :]
                high = value.astype(BF16)
                rest = (value - high.astype(F32)).astype(BF16)
                g_win[to, :] += nn(chosen, high) + nn(chosen, rest)

        return carry

    lax.fori_loop(0, info[OWN_N], place, 0)
    for win, parts in ((m_win, (m_left, m_own, m_right)), (g_win, (g_left, g_own, g_right))):
        for part, begin, size in ((parts[0], 0, HALO), (parts[1], HALO, tok), (parts[2], HALO + tok, HALO)):
            part[...] = win[pl.ds(begin, size), :].astype(part.dtype)


def unsort_rows(info, mixed, grad, tok):
    width = mixed.shape[1]
    smem = pl.BlockSpec(memory_space=pltpu.SMEM)
    vmem = pl.BlockSpec(memory_space=pltpu.VMEM)
    spare = tok + HALO + 288
    shapes = [
        jax.ShapeDtypeStruct((size, width), kind)
        for kind in (BF16, F32)
        for size in (tok, HALO, HALO)
    ]
    return pl.pallas_call(
        partial(unsort_kernel, tok),
        out_shape=shapes,
        in_specs=[smem, vmem, vmem],
        out_specs=[vmem] * 6,
        scratch_shapes=[pltpu.VMEM((spare, width), F32)] * 2,
        compiler_params=pltpu.CompilerParams(vmem_limit_bytes=VMEM),
        name="unsort_rows",
    )(info, mixed, grad)


def qkv_kernel(info, x, gain, shift, weight, bias, h_out, qkv_out):
    used = pl.program_id(0) * BLK < info[G_END]
    width = x.shape[1]

    @pl.when(used)
    def _():
        normed, _ = normalize(x[...].astype(F32))
        hidden = (normed * gain[...] + shift[...]).astype(BF16)
        h_out[...] = hidden
        for part in range(3):
            cols = pl.ds(part * width, width)
            value = nn(hidden, weight[:, cols]) + bias[:, cols]
            if part == 0:
                value = value * (HD ** (-0.5))
            qkv_out[:, cols] = value.astype(BF16)

    @pl.when(jnp.logical_not(used))
    def _():
        h_out[...] = jnp.zeros_like(h_out)
        qkv_out[...] = jnp.zeros_like(qkv_out)


def full(shape):
    return pl.BlockSpec(shape, lambda *_: (0,) * len(shape))


def held(shape):
    return pl.BlockSpec(shape, lambda *_: (0,) * len(shape), pipeline_mode=pl.Buffered(1))


SMEM_SPEC = pl.BlockSpec(memory_space=pltpu.SMEM)


def project_qkv(info, x, gain, shift, weight, bias):
    rows, width = x.shape
    return pl.pallas_call(
        qkv_kernel,
        grid=(rows // BLK,),
        out_shape=[
            jax.ShapeDtypeStruct((rows, width), BF16),
            jax.ShapeDtypeStruct((rows, 3 * width), BF16),
        ],
        in_specs=[
            SMEM_SPEC,
            pl.BlockSpec((BLK, width), lambda i: (i, 0)),
            full((1, width)),
            full((1, width)),
            held((width, 3 * width)),
            full((1, 3 * width)),
        ],
        out_specs=[
            pl.BlockSpec((BLK, width), lambda i: (i, 0)),
            pl.BlockSpec((BLK, 3 * width), lambda i: (i, 0)),
        ],
        compiler_params=pltpu.CompilerParams(vmem_limit_bytes=VMEM),
        name="project_qkv",
    )(info, x, gain, shift, weight, bias)


def softmax_rows(scores, keep):
    masked = jnp.where(keep, scores, NEG)
    expo = jnp.exp(masked - jnp.max(masked, axis=-1, keepdims=True))
    return expo / jnp.sum(expo, axis=-1, keepdims=True)


def for_items(info, visit):
    def image(index, carry):
        slot = SLOTS[0]
        keep = lax.broadcasted_iota(jnp.int32, (slot, slot), 1) < LENS[0]
        visit(pl.multiple_of(index * slot, 16), slot, keep)
        return carry

    def text(index, carry):
        slot = TXT_PAIR
        rows = lax.broadcasted_iota(jnp.int32, (slot, slot), 0) // TXT_LEN
        cols = lax.broadcasted_iota(jnp.int32, (slot, slot), 1) // TXT_LEN
        visit(pl.multiple_of(info[G_TXT] + index * slot, ROW), slot, rows == cols)
        return carry

    def both(index, carry):
        slot = SLOTS[2]
        real = index < info[N_BOTH]
        start = jnp.where(real, info[G_BOTH] + index * slot, info[G_PAD])
        size = jnp.where(real, LENS[2], info[PAD_LEN])
        keep = lax.broadcasted_iota(jnp.int32, (slot, slot), 1) < size
        visit(pl.multiple_of(start, 16), slot, keep)
        return carry

    lax.fori_loop(0, info[N_IMG], image, 0)
    lax.fori_loop(0, (info[N_TXT] + 1) // 2, text, 0)
    lax.fori_loop(0, info[N_BOTH] + info[N_PAD], both, 0)


def attend_kernel(info, query, key, value, out):
    out[...] = jnp.zeros_like(out)

    def visit(start, slot, keep):
        at = pl.ds(start, slot)
        q, k, v = query[at, :], key[at, :], value[at, :]
        first = lax.broadcasted_iota(jnp.int32, (1, 2 * HD), 1) < HD
        results = []
        for mine in (first, jnp.logical_not(first)):
            prob = softmax_rows(nt(jnp.where(mine, q, 0), k), keep)
            results.append(nn(prob.astype(BF16), v))
        out[at, :] = jnp.where(first, results[0], results[1]).astype(BF16)

    for_items(info, visit)


def attend(info, qkv):
    rows = qkv.shape[0]
    width = qkv.shape[1] // 3
    pairs = width // (2 * HD)
    cols = 2 * HD
    return pl.pallas_call(
        attend_kernel,
        grid=(pairs,),
        out_shape=jax.ShapeDtypeStruct((rows, width), BF16),
        in_specs=[
            SMEM_SPEC,
            pl.BlockSpec((rows, cols), lambda p: (0, p)),
            pl.BlockSpec((rows, cols), lambda p: (0, pairs + p)),
            pl.BlockSpec((rows, cols), lambda p: (0, 2 * pairs + p)),
        ],
        out_specs=pl.BlockSpec((rows, cols), lambda p: (0, p)),
        compiler_params=pltpu.CompilerParams(vmem_limit_bytes=VMEM),
        name="attend",
    )(info, qkv, qkv, qkv)


def attend_back_kernel(info, query, key, value, grad, dq_out, dk_out, dv_out):
    for out in (dq_out, dk_out, dv_out):
        out[...] = jnp.zeros_like(out)

    def visit(start, slot, keep):
        at = pl.ds(start, slot)
        q, k, v, g = query[at, :], key[at, :], value[at, :], grad[at, :]
        first = lax.broadcasted_iota(jnp.int32, (1, 2 * HD), 1) < HD
        dqs, dks, dvs = [], [], []
        for mine in (first, jnp.logical_not(first)):
            prob = softmax_rows(nt(jnp.where(mine, q, 0), k), keep)
            grad_prob = nt(jnp.where(mine, g, 0), v)
            inner = jnp.sum(prob * grad_prob, axis=-1, keepdims=True)
            grad_score = (prob * (grad_prob - inner)).astype(BF16)
            dqs.append(nn(grad_score, k))
            dks.append(tn(grad_score, q))
            dvs.append(tn(prob.astype(BF16), g))
        scale = HD ** (-0.5)
        dq = jnp.where(first, dqs[0], dqs[1]).astype(BF16)
        dq_out[at, :] = (dq.astype(F32) * scale).astype(BF16)
        dk_out[at, :] = jnp.where(first, dks[0], dks[1]).astype(BF16)
        dv_out[at, :] = jnp.where(first, dvs[0], dvs[1]).astype(BF16)

    for_items(info, visit)


def attend_back(info, qkv, grad):
    rows = qkv.shape[0]
    width = qkv.shape[1] // 3
    pairs = width // (2 * HD)
    cols = 2 * HD
    spec = pl.BlockSpec((rows, cols), lambda p: (0, p))
    return pl.pallas_call(
        attend_back_kernel,
        grid=(pairs,),
        out_shape=[jax.ShapeDtypeStruct((rows, width), BF16)] * 3,
        in_specs=[
            SMEM_SPEC,
            spec,
            pl.BlockSpec((rows, cols), lambda p: (0, pairs + p)),
            pl.BlockSpec((rows, cols), lambda p: (0, 2 * pairs + p)),
            spec,
        ],
        out_specs=[spec] * 3,
        compiler_params=pltpu.CompilerParams(vmem_limit_bytes=VMEM),
        name="attend_back",
    )(info, qkv, qkv, qkv, grad)


def group_of(info, row):
    return (
        (row >= info[G_TXT]).astype(jnp.int32)
        + (row >= info[G_BOTH]).astype(jnp.int32)
        + (row >= info[G_PAD]).astype(jnp.int32)
    )


def middle_kernel(info, x, att, grad, weight, bias, gains, shifts, mid_out, h_out, ht_out, gt_out):
    row = pl.program_id(0) * ROW
    used = row < info[G_END]

    @pl.when(used)
    def _():
        middle = x[...].astype(F32) + (nn(att[...], weight[...]) + bias[...])
        mid_out[...] = middle
        normed, _ = normalize(middle)
        which = pl.ds(group_of(info, row), 1)
        hidden = (normed * gains[which, :] + shifts[which, :]).astype(BF16)
        h_out[...] = hidden
        ht_out[...] = hidden.T
        gt_out[...] = grad[...].T

    @pl.when(jnp.logical_not(used))
    def _():
        mid_out[...] = jnp.zeros_like(mid_out)
        h_out[...] = jnp.zeros_like(h_out)
        ht_out[...] = jnp.zeros_like(ht_out)
        gt_out[...] = jnp.zeros_like(gt_out)


def middle_norm(info, x, att, grad, weight, bias, gains, shifts):
    rows, width = x.shape
    spec = pl.BlockSpec((ROW, width), lambda i: (i, 0))
    turned = pl.BlockSpec((width, ROW), lambda i: (0, i))
    return pl.pallas_call(
        middle_kernel,
        grid=(rows // ROW,),
        out_shape=[
            jax.ShapeDtypeStruct((rows, width), F32),
            jax.ShapeDtypeStruct((rows, width), BF16),
            jax.ShapeDtypeStruct((width, rows), BF16),
            jax.ShapeDtypeStruct((width, rows), BF16),
        ],
        in_specs=[
            SMEM_SPEC,
            spec,
            spec,
            spec,
            held((width, width)),
            full((1, width)),
            full(gains.shape),
            full(shifts.shape),
        ],
        out_specs=[spec, spec, turned, turned],
        compiler_params=pltpu.CompilerParams(vmem_limit_bytes=VMEM),
        name="middle_norm",
    )(info, x, att, grad, weight, bias, gains, shifts)


def gelu_parts(up):
    size = jnp.abs(up) * (0.5**0.5)
    expo = jnp.exp(-size * size)
    t = 1.0 / (1.0 + 0.3275911 * size)
    poly = 1.061405429 * t - 1.453152027
    poly = poly * t + 1.421413741
    poly = poly * t - 0.284496736
    poly = poly * t + 0.254829592
    tail = 0.5 * (poly * t) * expo
    cdf = jnp.where(up >= 0, 1.0 - tail, tail)
    return (up * cdf, cdf + up * (expo * 0.3989422804014327))


def expert_kernel(
    expert, info, h, ht, g, gt, w_up, b_up, w_down, y_in, d_in,
    grad_out, bias_out, y_out, d_out, act, dup, y_acc, d_acc, w_acc, sems,
):
    step = pl.program_id(0)
    steps = pl.num_programs(0)
    start = info[G_IMG + expert]
    count = info[G_IMG + expert + 1] - start
    blocks = count // BLK
    odd = count % BLK > 0
    bias_out[...] = jnp.zeros_like(bias_out)

    def rows_of(local, size):
        at = pl.ds(pl.multiple_of(start + local, ROW), size)
        here = pl.ds(pl.multiple_of(local, ROW), size)
        up = nn(h[at, :], w_up[0]) + b_up[0]
        grad_act = nt(g[at, :], w_down[0])
        active, slope = gelu_parts(up)
        active = active.astype(BF16)
        grad_up = (slope * grad_act).astype(BF16)
        act[here, :] = active
        dup[here, :] = grad_up
        bias_out[...] += jnp.sum(grad_up.astype(F32), axis=0, keepdims=True)
        y_part = nn(active, w_down[0])
        d_part = nt(grad_up, w_up[0])

        @pl.when(step == 0)
        def _():
            y_acc[here, :] = y_part
            d_acc[here, :] = d_part

        @pl.when(step > 0)
        def _():
            y_acc[here, :] += y_part
            d_acc[here, :] += d_part

    def block(index, carry):
        rows_of(index * BLK, BLK)
        return carry

    lax.fori_loop(0, blocks, block, 0)

    @pl.when(odd)
    def _():
        rows_of(blocks * BLK, ROW)

    for slot, (turned, right) in enumerate(((ht, dup), (gt, act))):
        w_acc[...] = jnp.zeros_like(w_acc)

        def add(local, size, turned=turned, right=right):
            at = pl.ds(pl.multiple_of(start + local, ROW), size)
            here = pl.ds(pl.multiple_of(local, ROW), size)
            w_acc[...] += nn(turned[:, at], right[here, :])

        def add_block(index, carry, add=add):
            add(index * BLK, BLK)
            return carry

        lax.fori_loop(0, blocks, add_block, 0)

        @pl.when(odd)
        def _(add=add):
            add(blocks * BLK, ROW)

        grad_out[slot] = w_acc[...].astype(BF16)

    @pl.when(step == steps - 1)
    def _():
        def copies(index):
            here = pl.ds(pl.multiple_of(index * ROW, ROW), ROW)
            at = pl.ds(pl.multiple_of(start + index * ROW, ROW), ROW)
            return (
                pltpu.make_async_copy(y_acc.at[here, :], y_out.at[at, :], sems.at[0, index]),
                pltpu.make_async_copy(d_acc.at[here, :], d_out.at[at, :], sems.at[1, index]),
            )

        def send(index, carry):
            for copy in copies(index):
                copy.start()
            return carry

        def wait(index, carry):
            for copy in copies(index):
                copy.wait()
            return carry

        lax.fori_loop(0, count // ROW, send, 0)
        lax.fori_loop(0, count // ROW, wait, 0)


def run_expert(expert, info, h, ht, g, gt, expert_up, up_bias, expert_down, y_buf, d_buf):
    rows, width = h.shape
    hidden = expert_up.shape[2]
    tile = min(hidden, 768)
    any_spec = pl.BlockSpec(memory_space=pl.ANY)
    return pl.pallas_call(
        partial(expert_kernel, expert),
        grid=(hidden // tile,),
        out_shape=[
            jax.ShapeDtypeStruct((2, width, hidden), BF16),
            jax.ShapeDtypeStruct((1, hidden), F32),
            jax.ShapeDtypeStruct((rows, width), F32),
            jax.ShapeDtypeStruct((rows, width), F32),
        ],
        in_specs=[
            SMEM_SPEC,
            held((rows, width)),
            held((width, rows)),
            held((rows, width)),
            held((width, rows)),
            pl.BlockSpec((1, width, tile), lambda f: (expert, 0, f)),
            pl.BlockSpec((1, 1, tile), lambda f: (expert, 0, f)),
            pl.BlockSpec((1, tile, width), lambda f: (expert, f, 0)),
            any_spec,
            any_spec,
        ],
        out_specs=[
            pl.BlockSpec((2, width, tile), lambda f: (0, 0, f)),
            pl.BlockSpec((1, tile), lambda f: (0, f)),
            any_spec,
            any_spec,
        ],
        scratch_shapes=[
            pltpu.VMEM((rows, tile), BF16),
            pltpu.VMEM((rows, tile), BF16),
            pltpu.VMEM((rows, width), F32),
            pltpu.VMEM((rows, width), F32),
            pltpu.VMEM((width, tile), F32),
            pltpu.SemaphoreType.DMA((2, rows // ROW)),
        ],
        input_output_aliases={8: 2, 9: 3},
        compiler_params=pltpu.CompilerParams(vmem_limit_bytes=VMEM),
        name="expert",
    )(info, h, ht, g, gt, expert_up, up_bias, expert_down, y_buf, d_buf)


def after_kernel(
    info, mid, y, dh, g, gains, down_bias, weight,
    mixed_out, dx_out, proj_out, att_out, gain_sum, shift_sum, down_sum, bias_sum,
):
    row = pl.program_id(0) * ROW
    used = row < info[G_END]

    @pl.when(row == 0)
    def _():
        for out in (gain_sum, shift_sum, down_sum, bias_sum):
            out[...] = jnp.zeros_like(out)

    @pl.when(used)
    def _():
        which = pl.ds(group_of(info, row), 1)
        middle = mid[...]
        grad = g[...].astype(F32)
        grad_hidden = dh[...]
        mixed_out[...] = (middle + (y[...] + down_bias[which, :])).astype(BF16)
        normed, inverse = normalize(middle)
        gain_sum[which, :] += jnp.sum(grad_hidden * normed, axis=0, keepdims=True)
        shift_sum[which, :] += jnp.sum(grad_hidden, axis=0, keepdims=True)
        down_sum[which, :] += jnp.sum(grad, axis=0, keepdims=True)
        grad_middle = grad + norm_back(grad_hidden * gains[which, :], normed, inverse)
        dx_out[...] = grad_middle
        proj = grad_middle.astype(BF16)
        proj_out[...] = proj
        bias_sum[...] += jnp.sum(proj.astype(F32), axis=0, keepdims=True)
        att_out[...] = nt(proj, weight[...]).astype(BF16)

    @pl.when(jnp.logical_not(used))
    def _():
        for out in (mixed_out, dx_out, proj_out, att_out):
            out[...] = jnp.zeros_like(out)


def after_experts(info, mid, y, dh, g, gains, down_bias, weight):
    rows, width = mid.shape
    spec = pl.BlockSpec((ROW, width), lambda i: (i, 0))
    sums = full((4, width))
    return pl.pallas_call(
        after_kernel,
        grid=(rows // ROW,),
        out_shape=[
            jax.ShapeDtypeStruct((rows, width), BF16),
            jax.ShapeDtypeStruct((rows, width), F32),
            jax.ShapeDtypeStruct((rows, width), BF16),
            jax.ShapeDtypeStruct((rows, width), BF16),
            jax.ShapeDtypeStruct((4, width), F32),
            jax.ShapeDtypeStruct((4, width), F32),
            jax.ShapeDtypeStruct((4, width), F32),
            jax.ShapeDtypeStruct((1, width), F32),
        ],
        in_specs=[SMEM_SPEC, spec, spec, spec, spec, sums, sums, held((width, width))],
        out_specs=[spec, spec, spec, spec, sums, sums, sums, full((1, width))],
        compiler_params=pltpu.CompilerParams(vmem_limit_bytes=VMEM),
        name="after_experts",
    )(info, mid, y, dh, g, gains, down_bias, weight)


def last_kernel(
    info, x, dx, dq, dk, dv, gain, weight, out, gain_sum, shift_sum, query_sum, value_sum
):
    width = x.shape[1]
    used = pl.program_id(0) * BLK < info[G_END]

    @pl.when(pl.program_id(0) == 0)
    def _():
        for total in (gain_sum, shift_sum, query_sum, value_sum):
            total[...] = jnp.zeros_like(total)

    @pl.when(used)
    def _():
        hidden = nt(dq[...], weight[:, pl.ds(0, width)])
        hidden += nt(dk[...], weight[:, pl.ds(width, width)])
        hidden += nt(dv[...], weight[:, pl.ds(2 * width, width)])
        normed, inverse = normalize(x[...].astype(F32))
        gain_sum[...] += jnp.sum(hidden * normed, axis=0, keepdims=True)
        shift_sum[...] += jnp.sum(hidden, axis=0, keepdims=True)
        query_sum[...] += jnp.sum(dq[...].astype(F32), axis=0, keepdims=True)
        value_sum[...] += jnp.sum(dv[...].astype(F32), axis=0, keepdims=True)
        out[...] = dx[...] + norm_back(hidden * gain[...], normed, inverse)

    @pl.when(jnp.logical_not(used))
    def _():
        out[...] = jnp.zeros_like(out)


def last_norm(info, x, dx, dq, dk, dv, gain, weight):
    rows, width = x.shape
    spec = pl.BlockSpec((BLK, width), lambda i: (i, 0))
    one = full((1, width))
    return pl.pallas_call(
        last_kernel,
        grid=(rows // BLK,),
        out_shape=[jax.ShapeDtypeStruct((rows, width), F32)]
        + [jax.ShapeDtypeStruct((1, width), F32)] * 4,
        in_specs=[SMEM_SPEC, spec, spec, spec, spec, spec, one, held((width, 3 * width))],
        out_specs=[spec, one, one, one, one],
        compiler_params=pltpu.CompilerParams(vmem_limit_bytes=VMEM),
        name="last_norm",
    )(info, x, dx, dq, dk, dv, gain, weight)


def low_add(a, b):
    return (a.astype(F32) + b.astype(F32)).astype(BF16)


def swap(value, bit):
    ways = lax.axis_size("dp")
    return lax.ppermute(value, "dp", [(i, i ^ (1 << bit)) for i in range(ways)])


def halve(parts, axis, bit):
    mine = (lax.axis_index("dp") >> bit) & 1

    def pick(which):
        taken = [lax.dynamic_index_in_dim(part, which, axis, keepdims=False) for part in parts]
        total = taken[0]
        for more in taken[1:]:
            total = low_add(total, more)
        return total

    send, keep = pick(1 - mine), pick(mine)
    return [keep, swap(send, bit)]


def scatter_sum(value):
    dp, seq = lax.axis_size("dp"), lax.axis_size("seq")
    bits = dp.bit_length() - 1
    two, depth, cols = value.shape
    rows = depth // (dp * seq)
    shaped = value.reshape((2,) + (2,) * bits + (seq, rows, cols))
    parts = halve([shaped], bits, 0)
    results = []
    for lane in range(2):
        lane_parts = [part[lane] for part in parts]
        order = list(range(1, bits))
        if lane:
            order = order[::-1]
        left = list(range(bits - 1, 0, -1))
        for bit in order:
            axis = left.index(bit)
            left.remove(bit)
            lane_parts = halve(lane_parts, axis, bit)
        results.append(low_add(lane_parts[0], lane_parts[1]))
    half = jnp.stack(results)
    here = lax.axis_index("seq")
    total = lax.dynamic_index_in_dim(half, here, 1, keepdims=False).astype(F32)
    for hop in range(1, seq):
        block = lax.dynamic_index_in_dim(half, (here + hop) % seq, 1, keepdims=False)
        got = lax.ppermute(block, "seq", [(i, (i + hop) % seq) for i in range(seq)])
        total = total + got.astype(F32)
    return total


def exchange(value, rows):
    seq = lax.axis_size("seq")
    from_left = lax.ppermute(value[-rows:], "seq", [(i, i + 1) for i in range(seq - 1)])
    from_right = lax.ppermute(value[:rows], "seq", [(i + 1, i) for i in range(seq - 1)])
    return (from_left, from_right)


def per_device(
    tokens, item_types, first_gain, first_shift, qkv_weight, query_bias, value_bias, attn_weight,
    attn_bias, second_gain, second_shift, expert_up, up_bias, expert_down, down_bias, cotangent,
):
    tok, width = tokens.shape
    seq = lax.axis_size("seq")
    rows = capacity(tok)
    place = lax.axis_index("seq").astype(jnp.int32).reshape(1)
    x_left, x_right = exchange(tokens, HALO)
    d_left, d_right = exchange(cotangent, HALO)
    x, g, info = sort_rows(
        place, item_types, (x_left, tokens, x_right), (d_left, cotangent, d_right), rows, tok, tok * seq
    )
    bias_full = jnp.concatenate([query_bias, jnp.zeros((width,), F32), value_bias])[None]
    pad_row = jnp.zeros((1, width), F32)
    gains = jnp.concatenate([second_gain, pad_row])
    shifts = jnp.concatenate([second_shift, pad_row])
    downs = jnp.concatenate([down_bias, pad_row])

    h, qkv = project_qkv(info, x, first_gain[None], first_shift[None], qkv_weight, bias_full)
    att = attend(info, qkv)
    mid, h2, h2t, gt = middle_norm(info, x, att, g, attn_weight, attn_bias[None], gains, shifts)

    y = jnp.zeros((rows, width), F32)
    dh = jnp.zeros((rows, width), F32)
    expert_sums, up_biases = [], []
    for expert in range(EXPERTS):
        grads, bias, y, dh = run_expert(
            expert, info, h2, h2t, g, gt, expert_up, up_bias[:, None, :], expert_down, y, dh
        )
        up_biases.append(bias)
        expert_sums.append(scatter_sum(grads))

    mixed, dx, proj, datt, gain_sum, shift_sum, down_sum, attn_bias_sum = after_experts(
        info, mid, y, dh, g, gains, downs, attn_weight
    )
    half = width // 2
    d_attn = tn(proj, att).astype(BF16)
    attn_sum = scatter_sum(jnp.stack([d_attn[:, :half], d_attn[:, half:]]))
    dq, dk, dv = attend_back(info, qkv, datt)
    grad_x, fgain, fshift, qsum, vsum = last_norm(
        info, x, dx, dq, dk, dv, first_gain[None], qkv_weight
    )
    d_qkv = jnp.concatenate([tn(dq, h), tn(dk, h), tn(dv, h)]).astype(BF16)
    qkv_sum = scatter_sum(jnp.stack([d_qkv[:, :half], d_qkv[:, half:]]))

    m_own, m_left, m_right, g_own, g_left, g_right = unsort_rows(info, mixed, grad_x, tok)

    def merge(own, left, right):
        to_left = lax.ppermute(left, "seq", [(i + 1, i) for i in range(seq - 1)])
        to_right = lax.ppermute(right, "seq", [(i, i + 1) for i in range(seq - 1)])
        own = own.at[:HALO].add(to_right)
        return own.at[tok - HALO :].add(to_left)

    mixed_out = merge(m_own, m_left, m_right)
    grad_out = merge(g_own, g_left, g_right)

    small = jnp.concatenate(
        [fgain[0], fshift[0], qsum[0], vsum[0], attn_bias_sum[0]]
        + [gain_sum[:EXPERTS].reshape(-1), shift_sum[:EXPERTS].reshape(-1), down_sum[:EXPERTS].reshape(-1)]
        + [bias[0] for bias in up_biases]
    )
    small = lax.psum(small, ("dp", "seq"))
    devices = lax.axis_size("dp") * seq
    own = width // devices
    rank = lax.axis_index("dp") * seq + lax.axis_index("seq")
    vectors = small[: 14 * width].reshape(14, width)
    vectors = lax.dynamic_slice_in_dim(vectors, rank * own, own, 1)
    sum_up = jnp.stack([total[0] for total in expert_sums])
    sum_down = jnp.stack([total[1] for total in expert_sums]).swapaxes(1, 2)

    def joined(total):
        return jnp.concatenate([total[0], total[1]], axis=1).T

    return (
        mixed_out,
        grad_out,
        vectors[0],
        vectors[1],
        joined(qkv_sum),
        vectors[2],
        vectors[3],
        joined(attn_sum),
        vectors[4],
        vectors[5:8],
        vectors[8:11],
        sum_up,
        small[14 * width :].reshape(EXPERTS, -1),
        sum_down,
        vectors[11:14],
    )


def solution(mesh):
    split = P(("dp", "seq"))
    in_specs = (P(("dp", "seq"), None), P("dp", None)) + (P(),) * 13 + (P(("dp", "seq"), None),)
    out_specs = (
        P(("dp", "seq"), None),
        P(("dp", "seq"), None),
        split,
        split,
        P(None, ("dp", "seq")),
        split,
        split,
        P(None, ("dp", "seq")),
        split,
        P(None, ("dp", "seq")),
        P(None, ("dp", "seq")),
        P(None, ("dp", "seq"), None),
        P(),
        P(None, None, ("dp", "seq")),
        P(None, ("dp", "seq")),
    )
    return jax.shard_map(
        per_device, mesh=mesh, in_specs=in_specs, out_specs=out_specs, check_vma=False
    )
```

time: 2530 us -> 740 us (0.29)
  waiting for transfers between devices: 1350 us -> 283 us
  matrix products: 589 us -> 14.1 us
  local copies, waits for them, and re-layouts: 353 us -> 53 us
  Pallas kernels: 0 us -> 259 us
  other arithmetic: 174 us -> 28.3 us
  starting transfers between devices: 22.4 us -> 84.1 us
    dot_general x85 -> x4, matrix products: 589 us -> 14.1 us  [tn(): lax.dot_general(a, b, (((0,), (0,)), ((), ())), preferred_element_type=F32)]
    unnamed x7 -> x1, waiting for transfers between devices: 518 us -> 0.02 us
    reduce_scatter x3 -> x0, waiting for transfers between devices: 496 us -> none  [the longest x1 269 us: per_device(): lax.psum_scatter(grad_up, ('dp', 'seq'), scatter_dimension=1, tiled=True)]
    all_to_all x4 -> x0, waiting for transfers between devices: 336 us -> none  [the longest x1 141 us: per_device(): lax.all_to_all(grad_stack, 'seq', split_axis=0, concat_axis=2, tiled=True)]
    pallas_call x0 -> x11, Pallas kernels: none -> 259 us  [the longest x3 98.6 us: run_expert(): pl.pallas_call(partial(expert_kernel, expert), grid=(hidden // tile,), ou...]
    ppermute x0 -> x48, waiting for transfers between devices: none -> 150 us  [the longest x25 98.5 us: swap(): return lax.ppermute(value, 'dp', [(i, i ^ 1 << bit) for i in range(ways)])]
    psum x0 -> x1, waiting for transfers between devices: none -> 133 us  [per_device(): small = lax.psum(small, ('dp', 'seq'))]
    dynamic_update_slice x24 -> x0, local copies, waits for them, and re-layouts: 131 us -> none  [the longest x8 63.3 us: grad_block(): lax.dynamic_update_slice_in_dim(grad_keys, lax.dynamic_slice_in_dim(grad_...]
  transfers between devices with their start and end apart: 9 -> 49, of which waited for: 8 -> 25; matrix products, arithmetic and copies ran while one was open for 9% -> 8% of each run, Pallas kernels for 0% -> 12%
where the time goes in v1:
time: 740 us; the launch traced here: 737 us
  waiting for transfers between devices  283 us (38%)
  Pallas kernels  259 us (35%)
  starting transfers between devices  84.1 us (11%)
  local copies, waits for them, and re-layouts  53 us (7%)
  other arithmetic  28.3 us (4%)
  between operations  15.6 us (2%)
  matrix products  14.1 us (2%)
    psum x1, waiting for transfers between devices, per_device(): small = lax.psum(small, ('dp', 'seq'))  133 us
    pallas_call x3, Pallas kernels, run_expert(): pl.pallas_call(partial(expert_kernel, expert), grid=(hidden // tile,), ou...  98.6 us
    ppermute x25, waiting for transfers between devices, swap(): return lax.ppermute(value, 'dp', [(i, i ^ 1 << bit) for i in range(ways)])  98.5 us
    pallas_call x1, Pallas kernels, attend_back(): pl.pallas_call(attend_back_kernel, grid=(pairs,), out_shape=[jax.ShapeDty...  45.4 us
    ppermute x15, starting transfers between devices, scatter_sum(): got = lax.ppermute(block, 'seq', [(i, (i + hop) % seq) for i in range(seq)])  39.3 us
    ppermute x15, waiting for transfers between devices, scatter_sum(): got = lax.ppermute(block, 'seq', [(i, (i + hop) % seq) for i in range(seq)])  39.3 us
    pallas_call x1, Pallas kernels, attend(): pl.pallas_call(attend_kernel, grid=(pairs,), out_shape=jax.ShapeDtypeStru...  31.2 us
    ppermute x25, starting transfers between devices, swap(): return lax.ppermute(value, 'dp', [(i, i ^ 1 << bit) for i in range(ways)])  24.9 us
  transfers between devices with their start and end apart: 49, of which 25 were waited for; matrix products, arithmetic and copies ran while one was open for 8% of the time, Pallas kernels for 12%

profile of v1, /device:TPU:0, one launch (start us, length us, event | category | flops | bytes accessed | tf_op | source)
XLA Modules:
  0.0 737.2 jit_solution(12277402162316580735)
XLA Ops:
  8.4 4.9 collective-permute-start
  15.7 4.6 collective-permute-start.2
  29.2 12.0 %sort_rows.1 = (bf16[1792,768]{1,0:T(8,128)(2,1)}, bf16[1792,768]{1,0:T(8,128)(2,1)}, s32[256]{0:T(256)}) custom-call(s32[1]{0:T(128)} %bitcast.pos, s32[1,64]{1,0:T(1,128)} %types.1, bf16[144,768]{1,0:T(8,128)(2,1)} %copy-done.6, bf16[1024,768]{1,0:T(8,128)(2,1)} %x_own.1, bf16[144,768]{1,0:T(8,128)(2,1)} %copy-done.7, bf16[144,768]{1,0:T(8,128)(2,1)} %copy-done.8, ...), custom_call_target="tpu_custom_call" | custom-call | tf_op jit(solution)/shard_map/sort_rows/pallas_call | solution.py:201
  41.2 11.6 %project_qkv.1 = (bf16[1792,768]{1,0:T(8,128)(2,1)}, bf16[1792,2304]{1,0:T(8,128)(2,1)}) custom-call(s32[256]{0:T(256)} %get-tuple-element.106.info, bf16[1792,768]{1,0:T(8,128)(2,1)} %get-tuple-element.107.x, f32[1,768]{1,0:T(1,128)} %broadcast_in_dim.22.gain, f32[1,768]{1,0:T(1,128)} %broadcast_in_dim.23.shift, bf16[768,2304]{1,0:T(8,128)(2,1)} %weight.7, ...), custom_call_target="tpu_custom_call" | custom-call | tf_op jit(solution)/shard_map/project_qkv/pallas_call | solution.py:307
  52.7 31.2 %attend.1.att = bf16[1792,768]{1,0:T(8,128)(2,1)} custom-call(s32[256]{0:T(256)} %get-tuple-element.106.info, bf16[1792,2304]{1,0:T(8,128)(2,1)} %get-tuple-element.108.query.key.value, bf16[1792,2304]{1,0:T(8,128)(2,1)} %get-tuple-element.108.query.key.value, bf16[1792,2304]{1,0:T(8,128)(2,1)} %get-tuple-element.108.query.key.value), custom_call_target="tpu_custom_call" | custom-call | tf_op jit(solution)/shard_map/attend/pallas_call | solution.py:386
  84.0 15.7 %middle_norm.1 = (f32[1792,768]{1,0:T(8,128)}, bf16[1792,768]{1,0:T(8,128)(2,1)}, bf16[768,1792]{1,0:T(8,128)(2,1)}, bf16[768,1792]{1,0:T(8,128)(2,1)}) custom-call(s32[256]{0:T(256)} %get-tuple-element.106.info, bf16[1792,768]{1,0:T(8,128)(2,1)} %get-tuple-element.107.x, bf16[1792,768]{1,0:T(8,128)(2,1)} %attend.1.att, ...), custom_call_target="tpu_custom_call" | custom-call | tf_op jit(solution)/shard_map/middle_norm/pallas_call | solution.py:486
  99.7 2.8 broadcast_1_y_in_d_in.2.y_in
  102.5 2.7 broadcast_1_y_in_d_in.2.clone.d_in
  105.2 35.1 %expert.3 = (bf16[2,768,3072]{2,1,0:T(8,128)(2,1)}, f32[1,3072]{1,0:T(1,128)}, f32[1792,768]{1,0:T(8,128)}, f32[1792,768]{1,0:T(8,128)}) custom-call(s32[256]{0:T(256)} %get-tuple-element.106.info, bf16[1792,768]{1,0:T(8,128)(2,1)} %get-tuple-element.111.h, bf16[768,1792]{1,0:T(8,128)(2,1)} %get-tuple-element.112.ht, ...), custom_call_target="tpu_custom_call", output_to_operand_aliasing={{2}: (8, {}), {3}: (9, {})} | custom-call | tf_op jit(solution)/shard_map/expert/pallas_call | solution.py:619
  140.3 5.0 copy_bitcast_fusion.2
  145.4 3.2 dynamic-slice_bitcast_fusion.2
  148.6 19.4 %expert.4 = (bf16[2,768,3072]{2,1,0:T(8,128)(2,1)}, f32[1,3072]{1,0:T(1,128)}, f32[1792,768]{1,0:T(8,128)}, f32[1792,768]{1,0:T(8,128)}) custom-call(s32[256]{0:T(256)} %get-tuple-element.106.info, bf16[1792,768]{1,0:T(8,128)(2,1)} %get-tuple-element.111.h, bf16[768,1792]{1,0:T(8,128)(2,1)} %get-tuple-element.112.ht, ...), custom_call_target="tpu_custom_call", output_to_operand_aliasing={{2}: (8, {}), {3}: (9, {})} | custom-call | tf_op jit(solution)/shard_map/expert/pallas_call | solution.py:619
  168.0 4.9 copy_bitcast_fusion.1
  173.0 3.3 dynamic-slice_bitcast_fusion.1
  176.3 44.0 %expert.5 = (bf16[2,768,3072]{2,1,0:T(8,128)(2,1)}, f32[1,3072]{1,0:T(1,128)}, f32[1792,768]{1,0:T(8,128)}, f32[1792,768]{1,0:T(8,128)}) custom-call(s32[256]{0:T(256)} %get-tuple-element.106.info, bf16[1792,768]{1,0:T(8,128)(2,1)} %get-tuple-element.111.h, bf16[768,1792]{1,0:T(8,128)(2,1)} %get-tuple-element.112.ht, ...), custom_call_target="tpu_custom_call", output_to_operand_aliasing={{2}: (8, {}), {3}: (9, {})} | custom-call | tf_op jit(solution)/shard_map/expert/pallas_call | solution.py:619
  220.3 4.9 copy_bitcast_fusion
  225.2 3.3 dynamic-slice_bitcast_fusion
  229.0 19.8 %after_experts.1 = (bf16[1792,768]{1,0:T(8,128)(2,1)}, f32[1792,768]{1,0:T(8,128)}, bf16[1792,768]{1,0:T(8,128)(2,1)}, bf16[1792,768]{1,0:T(8,128)(2,1)}, f32[4,...) custom-call(s32[256]{0:T(256)} %get-tuple-element.106.info, ...), custom_call_target="tpu_custom_call" | custom-call | tf_op jit(solution)/shard_map/after_experts/pallas_call | solution.py:700
  248.8 4.1 convolution_convert_fusion
  254.1 45.4 %attend_back.1 = (bf16[1792,768]{1,0:T(8,128)(2,1)}, bf16[1792,768]{1,0:T(8,128)(2,1)}, bf16[1792,768]{1,0:T(8,128)(2,1)}) custom-call(s32[256]{0:T(256)} %get-tuple-element.106.info, bf16[1792,2304]{1,0:T(8,128)(2,1)} %get-tuple-element.108.query.key.value, bf16[1792,2304]{1,0:T(8,128)(2,1)} %get-tuple-element.108.query.key.value, ...), custom_call_target="tpu_custom_call" | custom-call | tf_op jit(solution)/shard_map/attend_back/pallas_call | solution.py:434
  299.5 5.1 convolution_convert_fusion.1
  314.4 14.7 %last_norm.1 = (f32[1792,768]{1,0:T(8,128)}, f32[1,768]{1,0:T(1,128)}, f32[1,768]{1,0:T(1,128)}, f32[1,768]{1,0:T(1,128)}, f32[1,768]{1,0:T(1,128)}) custom-call(s32[256]{0:T(256)} %get-tuple-element.106.info, bf16[1792,768]{1,0:T(8,128)(2,1)} %get-tuple-element.107.x, f32[1792,768]{1,0:T(8,128)} %get-tuple-element.121.dx, ...), custom_call_target="tpu_custom_call" | custom-call | tf_op jit(solution)/shard_map/last_norm/pallas_call | solution.py:752
  332.9 10.1 %unsort_rows.1 = (bf16[1024,768]{1,0:T(8,128)(2,1)}, bf16[144,768]{1,0:T(8,128)(2,1)}, bf16[144,768]{1,0:T(8,128)(2,1)}, f32[1024,768]{1,0:T(8,128)}, f32[144,768]{1,0:T(8,128)}, /*index=5*/f32[144,768]{1,0:T(8,128)}) custom-call(s32[256]{0:T(256)} %get-tuple-element.106.info, bf16[1792,768]{1,0:T(8,128)(2,1)} %get-tuple-element.120.mixed, ...), custom_call_target="tpu_custom_call" | custom-call | tf_op jit(solution)/shard_map/unsort_rows/pallas_call | solution.py:261
  344.3 133.3 %all-reduce.5.cloned.1.call-done = f32[19968]{0:T(1024)} async-done(((f32[19968]{0:T(1024)}), f32[19968]{0:T(1024)}) %all-reduce.5.cloned.1.call-update) | async-done | bytes 79888 | tf_op jit(solution)/shard_map/psum | solution.py:885
  484.1 7.4 %collective-permute-done.5 = bf16[144,768]{1,0:T(8,128)(2,1)S(1)} collective-permute-done((bf16[144,768]{1,0:T(8,128)(2,1)}, bf16[144,768]{1,0:T(8,128)(2,1)S(1)}, u32[]{:S(2)}, u32[]{:S(2)}) %collective-permute-start.5) | collective-permute-done | bytes 221216 | tf_op jit(solution)/shard_map/ppermute | solution.py:872
  491.5 3.9 collective-permute-start.6
  508.2 2.8 collective-permute-done.20
  512.6 3.7 collective-permute-done.18
  520.0 3.2 collective-permute-start.21
  528.9 3.4 collective-permute-start.23
  536.2 4.2 collective-permute-done.12
  542.5 3.0 collective-permute-start.14
  545.5 3.0 collective-permute-done.13
  548.5 2.8 collective-permute-start.15
  554.4 2.7 fusion.119
  562.9 2.7 fusion.120
  571.8 2.7 fusion.1
  577.4 11.3 %collective-permute-done.27 = bf16[2,4,24,3072]{3,2,1,0:T(8,128)(2,1)S(1)} collective-permute-done((bf16[2,4,24,3072]{3,2,1,0:T(8,128)(2,1)S(1)}, bf16[2,4,24,3072]{3,2,1,0:T(8,128)(2,1)S(1)}, u32[]{:S(2)}, u32[]{:S(2)}) %collective-permute-start.27) | collective-permute-done | bytes 1179680 | tf_op jit(solution)/shard_map/ppermute | solution.py:770
  591.9 22.1 %collective-permute-done.35 = bf16[2,4,24,3072]{3,2,1,0:T(8,128)(2,1)S(1)} collective-permute-done((bf16[2,4,24,3072]{3,2,1,0:T(8,128)(2,1)S(1)}, bf16[2,4,24,3072]{3,2,1,0:T(8,128)(2,1)S(1)}, u32[]{:S(2)}, u32[]{:S(2)}) %collective-permute-start.35) | collective-permute-done | bytes 1179680 | tf_op jit(solution)/shard_map/ppermute | solution.py:770
  617.2 22.1 %collective-permute-done.43 = bf16[2,4,24,3072]{3,2,1,0:T(8,128)(2,1)S(1)} collective-permute-done((bf16[2,4,24,3072]{3,2,1,0:T(8,128)(2,1)S(1)}, bf16[2,4,24,3072]{3,2,1,0:T(8,128)(2,1)S(1)}, u32[]{:S(2)}, u32[]{:S(2)}) %collective-permute-start.43) | collective-permute-done | bytes 1179680 | tf_op jit(solution)/shard_map/ppermute | solution.py:770
  642.5 12.5 %collective-permute-done.28 = bf16[4,24,3072]{2,1,0:T(8,128)(2,1)S(1)} collective-permute-done((bf16[4,24,3072]{2,1,0:T(8,128)(2,1)S(1)}, bf16[4,24,3072]{2,1,0:T(8,128)(2,1)S(1)}, u32[]{:S(2)}, u32[]{:S(2)}) %collective-permute-start.28) | collective-permute-done | bytes 589856 | tf_op jit(solution)/shard_map/ppermute | solution.py:770
  655.6 12.0 %collective-permute-done.36 = bf16[4,24,3072]{2,1,0:T(8,128)(2,1)S(1)} collective-permute-done((bf16[4,24,3072]{2,1,0:T(8,128)(2,1)S(1)}, bf16[4,24,3072]{2,1,0:T(8,128)(2,1)S(1)}, u32[]{:S(2)}, u32[]{:S(2)}) %collective-permute-start.36) | collective-permute-done | bytes 589856 | tf_op jit(solution)/shard_map/ppermute | solution.py:770
  669.6 4.5 collective-permute-done.44
  679.3 15.7 %collective-permute-done.30 = bf16[2,24,3072]{2,1,0:T(8,128)(2,1)S(1)} collective-permute-done((bf16[2,24,3072]{2,1,0:T(8,128)(2,1)S(1)}, bf16[2,24,3072]{2,1,0:T(8,128)(2,1)S(1)}, u32[]{:S(2)}, u32[]{:S(2)}) %collective-permute-start.30) | collective-permute-done | bytes 294944 | tf_op jit(solution)/shard_map/ppermute | solution.py:811
  695.0 13.6 %collective-permute-start.46 = (bf16[2,24,3072]{2,1,0:T(8,128)(2,1)S(1)}, bf16[2,24,3072]{2,1,0:T(8,128)(2,1)S(1)}, u32[]{:S(2)}, u32[]{:S(2)}) collective-permute-start(bf16[2,24,3072]{2,1,0:T(8,128)(2,1)S(1)} %get-tuple-element.190), channel_id=1, source_target_pairs={{0,2},{1,3},{2,0},{3,1},{4,6},{5,7},{6,4},{7,5},{8,10},{9,11},{10,... | collective-permute-start | bytes 884744 | tf_op jit(solution)/shard_map/ppermute | solution.py:811
  708.8 3.4 collective-permute-start.47
  712.2 6.3 collective-permute-done.38
  718.7 9.8 %collective-permute-done.46 = bf16[2,24,3072]{2,1,0:T(8,128)(2,1)S(1)} collective-permute-done((bf16[2,24,3072]{2,1,0:T(8,128)(2,1)S(1)}, bf16[2,24,3072]{2,1,0:T(8,128)(2,1)S(1)}, u32[]{:S(2)}, u32[]{:S(2)}) %collective-permute-start.46) | collective-permute-done | bytes 294944 | tf_op jit(solution)/shard_map/ppermute | solution.py:811
  (241 shorter events, 101.8 us)
Async XLA Ops:
  7.3 470.4 %all-reduce.5.cloned.1.call-start = ((), (), s32[]{:S(2)}) async-start(), calls=%async_computation | async-start | bytes 163840 | tf_op jit(solution)/shard_map/psum | solution.py:885
  8.4 18.1 %collective-permute-start = (bf16[144,768]{1,0:T(8,128)(2,1)S(1)}, bf16[144,768]{1,0:T(8,128)(2,1)S(1)}, u32[]{:S(2)}, u32[]{:S(2)}) collective-permute-start(bf16[144,768]{1,0:T(8,128)(2,1)S(1)} %get-tuple-element.182), channel_id=1, source_target_pairs={{0,1},{1,2},{2,3},{4,5},{5,6},{6,7},{8,9},{9,10},{10,11},{12,13},{... | collective-permute-start | bytes 663560 | tf_op jit(solution)/shard_map/ppermute | solution.py:818
  13.4 13.2 %collective-permute-start.1 = (bf16[144,768]{1,0:T(8,128)(2,1)S(1)}, bf16[144,768]{1,0:T(8,128)(2,1)S(1)}, u32[]{:S(2)}, u32[]{:S(2)}) collective-permute-start(bf16[144,768]{1,0:T(8,128)(2,1)S(1)} %get-tuple-element.181), channel_id=1, source_target_pairs={{1,0},{2,1},{3,2},{5,4},{6,5},{7,6},{9,8},{10,9},{11,10},{13,12},{... | collective-permute-start | bytes 663560 | tf_op jit(solution)/shard_map/ppermute | solution.py:819
  15.7 10.8 %collective-permute-start.2 = (bf16[144,768]{1,0:T(8,128)(2,1)S(1)}, bf16[144,768]{1,0:T(8,128)(2,1)S(1)}, u32[]{:S(2)}, u32[]{:S(2)}) collective-permute-start(bf16[144,768]{1,0:T(8,128)(2,1)S(1)} %get-tuple-element.180), channel_id=1, source_target_pairs={{0,1},{1,2},{2,3},{4,5},{5,6},{6,7},{8,9},{9,10},{10,11},{12,13},{... | collective-permute-start | bytes 663560 | tf_op jit(solution)/shard_map/ppermute | solution.py:818
  20.3 8.2 %collective-permute-start.3 = (bf16[144,768]{1,0:T(8,128)(2,1)S(1)}, bf16[144,768]{1,0:T(8,128)(2,1)S(1)}, u32[]{:S(2)}, u32[]{:S(2)}) collective-permute-start(bf16[144,768]{1,0:T(8,128)(2,1)S(1)} %get-tuple-element.179), channel_id=1, source_target_pairs={{1,0},{2,1},{3,2},{5,4},{6,5},{7,6},{9,8},{10,9},{11,10},{13,12},{... | collective-permute-start | bytes 663560 | tf_op jit(solution)/shard_map/ppermute | solution.py:819
  228.5 325.9 %collective-permute-start.24 = (bf16[2,2,2,4,24,3072]{5,4,3,1,2,0:T(8,128)(2,1)}, bf16[2,2,2,4,24,3072]{5,4,3,1,2,0:T(8,128)(2,1)}, u32[]{:S(2)}, u32[]{:S(2)}) collective-permute-start(bf16[2,2,2,4,24,3072]{5,4,3,1,2,0:T(8,128)(2,1)} %copy_bitcast_fusion.2), channel_id=1, source_target_pairs={{0,4},{4,0},{8,12},{12,8},{16,20},{20,16},{24,28},{28,24},{1,5},{5... | collective-permute-start | bytes 14155784 | tf_op jit(solution)/shard_map/ppermute | solution.py:770
  228.5 334.4 %collective-permute-start.32 = (bf16[2,2,2,4,24,3072]{5,4,3,1,2,0:T(8,128)(2,1)}, bf16[2,2,2,4,24,3072]{5,4,3,1,2,0:T(8,128)(2,1)}, u32[]{:S(2)}, u32[]{:S(2)}) collective-permute-start(bf16[2,2,2,4,24,3072]{5,4,3,1,2,0:T(8,128)(2,1)} %copy_bitcast_fusion.1), channel_id=1, source_target_pairs={{0,4},{4,0},{8,12},{12,8},{16,20},{20,16},{24,28},{28,24},{1,5},{5... | collective-permute-start | bytes 14155784 | tf_op jit(solution)/shard_map/ppermute | solution.py:770
  254.1 243.1 %collective-permute-start.16 = (bf16[2,2,2,4,24,384]{5,4,3,1,2,0:T(8,128)(2,1)}, bf16[2,2,2,4,24,384]{5,4,3,1,2,0:T(8,128)(2,1)S(1)}, u32[]{:S(2)}, u32[]{:S(2)}) collective-permute-start(bf16[2,2,2,4,24,384]{5,4,3,1,2,0:T(8,128)(2,1)} %bitcast.435), channel_id=1, source_target_pairs={{0,4},{4,0},{8,12},{12,8},{16,20},{20,16},{24,28},{28,24},{1,5},{5... | collective-permute-start | bytes 1769480 | tf_op jit(solution)/shard_map/ppermute | solution.py:770
  312.1 204.2 %collective-permute-start.8 = (bf16[2,2,2,4,72,384]{5,4,3,1,2,0:T(8,128)(2,1)}, bf16[2,2,2,4,72,384]{5,4,3,1,2,0:T(8,128)(2,1)}, u32[]{:S(2)}, u32[]{:S(2)}) collective-permute-start(bf16[2,2,2,4,72,384]{5,4,3,1,2,0:T(8,128)(2,1)} %bitcast.434), channel_id=1, source_target_pairs={{0,4},{4,0},{8,12},{12,8},{16,20},{20,16},{24,28},{28,24},{1,5},{5... | collective-permute-start | bytes 5308424 | tf_op jit(solution)/shard_map/ppermute | solution.py:770
  343.0 138.1 %collective-permute-start.4 = (bf16[144,768]{1,0:T(8,128)(2,1)}, bf16[144,768]{1,0:T(8,128)(2,1)S(1)}, u32[]{:S(2)}, u32[]{:S(2)}) collective-permute-start(bf16[144,768]{1,0:T(8,128)(2,1)} %get-tuple-element.128), channel_id=1, source_target_pairs={{0,1},{1,2},{2,3},{4,5},{5,6},{6,7},{8,9},{9,10},{10,11},{12,13},{... | collective-permute-start | bytes 663560 | tf_op jit(solution)/shard_map/ppermute | solution.py:873
  481.2 10.4 %collective-permute-start.5 = (bf16[144,768]{1,0:T(8,128)(2,1)}, bf16[144,768]{1,0:T(8,128)(2,1)S(1)}, u32[]{:S(2)}, u32[]{:S(2)}) collective-permute-start(bf16[144,768]{1,0:T(8,128)(2,1)} %get-tuple-element.129), channel_id=1, source_target_pairs={{1,0},{2,1},{3,2},{5,4},{6,5},{7,6},{9,8},{10,9},{11,10},{13,12},{... | collective-permute-start | bytes 663560 | tf_op jit(solution)/shard_map/ppermute | solution.py:872
  491.5 10.0 %collective-permute-start.6 = (f32[144,768]{1,0:T(8,128)}, f32[144,768]{1,0:T(8,128)S(1)}, u32[]{:S(2)}, u32[]{:S(2)}) collective-permute-start(f32[144,768]{1,0:T(8,128)} %get-tuple-element.131), channel_id=1, source_target_pairs={{0,1},{1,2},{2,3},{4,5},{5,6},{6,7},{8,9},{9,10},{10,11},{12,13},{... | collective-permute-start | bytes 1327112 | tf_op jit(solution)/shard_map/ppermute | solution.py:873
  497.3 7.6 %collective-permute-start.19 = (bf16[2,4,24,384]{3,2,1,0:T(8,128)(2,1)S(1)}, bf16[2,4,24,384]{3,2,1,0:T(8,128)(2,1)S(1)}, u32[]{:S(2)}, u32[]{:S(2)}) collective-permute-start(bf16[2,4,24,384]{3,2,1,0:T(8,128)(2,1)S(1)} %get-tuple-element.203), channel_id=1, source_target_pairs={{0,16},{4,20},{8,24},{12,28},{16,0},{20,4},{24,8},{28,12},{1,17},{... | collective-permute-start | bytes 442376 | tf_op jit(solution)/shard_map/ppermute | solution.py:770
  501.6 5.1 collective-permute-start.17
  504.9 18.5 %collective-permute-start.7 = (f32[144,768]{1,0:T(8,128)S(1)}, f32[144,768]{1,0:T(8,128)S(1)}, u32[]{:S(2)}, u32[]{:S(2)}) collective-permute-start(f32[144,768]{1,0:T(8,128)S(1)} %copy-done.28), channel_id=1, source_target_pairs={{1,0},{2,1},{3,2},{5,4},{6,5},{7,6},{9,8},{10,9},{11,10},{13,12},{... | collective-permute-start | bytes 1327112 | tf_op jit(solution)/shard_map/ppermute | solution.py:872
  511.1 5.2 collective-permute-start.18
  518.4 10.6 %collective-permute-start.11 = (bf16[2,4,72,384]{3,2,1,0:T(8,128)(2,1)S(1)}, bf16[2,4,72,384]{3,2,1,0:T(8,128)(2,1)S(1)}, u32[]{:S(2)}, u32[]{:S(2)}) collective-permute-start(bf16[2,4,72,384]{3,2,1,0:T(8,128)(2,1)S(1)} %get-tuple-element.172), channel_id=1, source_target_pairs={{0,16},{4,20},{8,24},{12,28},{16,0},{20,4},{24,8},{28,12},{1,17},{... | collective-permute-start | bytes 1327112 | tf_op jit(solution)/shard_map/ppermute | solution.py:770
  520.0 6.8 collective-permute-start.21
  523.4 11.1 %collective-permute-start.9 = (bf16[2,4,72,384]{3,2,1,0:T(8,128)(2,1)S(1)}, bf16[2,4,72,384]{3,2,1,0:T(8,128)(2,1)S(1)}, u32[]{:S(2)}, u32[]{:S(2)}) collective-permute-start(bf16[2,4,72,384]{3,2,1,0:T(8,128)(2,1)S(1)} %get-tuple-element.178), channel_id=1, source_target_pairs={{0,8},{4,12},{8,0},{12,4},{16,24},{20,28},{24,16},{28,20},{1,9},{5... | collective-permute-start | bytes 1327112 | tf_op jit(solution)/shard_map/ppermute | solution.py:770
  526.7 5.7 collective-permute-start.22
  528.9 5.1 collective-permute-start.23
  532.5 38.9 %collective-permute-start.40 = (bf16[2,2,2,4,24,3072]{5,4,3,1,2,0:T(8,128)(2,1)S(1)}, bf16[2,2,2,4,24,3072]{5,4,3,1,2,0:T(8,128)(2,1)S(1)}, u32[]{:S(2)}, u32[]{:S(2)}) collective-permute-start(bf16[2,2,2,4,24,3072]{5,4,3,1,2,0:T(8,128)(2,1)S(1)} %bitcast.451), channel_id=1, source_target_pairs={{0,4},{4,0},{8,12},{12,8},{16,20},{20,16},{24,28},{28,24},{1,5},{5... | collective-permute-start | bytes 14155784 | tf_op jit(solution)/shard_map/ppermute | solution.py:770
  534.0 6.4 collective-permute-start.12
  534.6 6.2 collective-permute-start.10
  541.0 7.6 %collective-permute-start.13 = (bf16[2,72,384]{2,1,0:T(8,128)(2,1)S(1)}, bf16[2,72,384]{2,1,0:T(8,128)(2,1)S(1)}, u32[]{:S(2)}, u32[]{:S(2)}) collective-permute-start(bf16[2,72,384]{2,1,0:T(8,128)(2,1)S(1)} %get-tuple-element.210), channel_id=1, source_target_pairs={{0,1},{1,2},{2,3},{3,0},{4,5},{5,6},{6,7},{7,4},{8,9},{9,10},{10,1... | collective-permute-start | bytes 331784 | tf_op jit(solution)/shard_map/ppermute | solution.py:811
  542.5 9.4 %collective-permute-start.14 = (bf16[2,72,384]{2,1,0:T(8,128)(2,1)S(1)}, bf16[2,72,384]{2,1,0:T(8,128)(2,1)S(1)}, u32[]{:S(2)}, u32[]{:S(2)}) collective-permute-start(bf16[2,72,384]{2,1,0:T(8,128)(2,1)S(1)} %get-tuple-element.211), channel_id=1, source_target_pairs={{0,2},{1,3},{2,0},{3,1},{4,6},{5,7},{6,4},{7,5},{8,10},{9,11},{10,... | collective-permute-start | bytes 331784 | tf_op jit(solution)/shard_map/ppermute | solution.py:811
  548.5 5.1 collective-permute-start.15
  559.8 29.0 %collective-permute-start.27 = (bf16[2,4,24,3072]{3,2,1,0:T(8,128)(2,1)S(1)}, bf16[2,4,24,3072]{3,2,1,0:T(8,128)(2,1)S(1)}, u32[]{:S(2)}, u32[]{:S(2)}) collective-permute-start(bf16[2,4,24,3072]{3,2,1,0:T(8,128)(2,1)S(1)} %get-tuple-element.150), channel_id=1, source_target_pairs={{0,16},{4,20},{8,24},{12,28},{16,0},{20,4},{24,8},{28,12},{1,17},{... | collective-permute-start | bytes 3538952 | tf_op jit(solution)/shard_map/ppermute | solution.py:770
  562.8 29.0 %collective-permute-start.25 = (bf16[2,4,24,3072]{3,2,1,0:T(8,128)(2,1)S(1)}, bf16[2,4,24,3072]{3,2,1,0:T(8,128)(2,1)S(1)}, u32[]{:S(2)}, u32[]{:S(2)}) collective-permute-start(bf16[2,4,24,3072]{3,2,1,0:T(8,128)(2,1)S(1)} %get-tuple-element.158), channel_id=1, source_target_pairs={{0,8},{4,12},{8,0},{12,4},{16,24},{20,28},{24,16},{28,20},{1,9},{5... | collective-permute-start | bytes 3538952 | tf_op jit(solution)/shard_map/ppermute | solution.py:770
  568.3 45.7 %collective-permute-start.35 = (bf16[2,4,24,3072]{3,2,1,0:T(8,128)(2,1)S(1)}, bf16[2,4,24,3072]{3,2,1,0:T(8,128)(2,1)S(1)}, u32[]{:S(2)}, u32[]{:S(2)}) collective-permute-start(bf16[2,4,24,3072]{3,2,1,0:T(8,128)(2,1)S(1)} %get-tuple-element.152), channel_id=1, source_target_pairs={{0,16},{4,20},{8,24},{12,28},{16,0},{20,4},{24,8},{28,12},{1,17},{... | collective-permute-start | bytes 3538952 | tf_op jit(solution)/shard_map/ppermute | solution.py:770
  571.2 45.8 %collective-permute-start.33 = (bf16[2,4,24,3072]{3,2,1,0:T(8,128)(2,1)S(1)}, bf16[2,4,24,3072]{3,2,1,0:T(8,128)(2,1)S(1)}, u32[]{:S(2)}, u32[]{:S(2)}) collective-permute-start(bf16[2,4,24,3072]{3,2,1,0:T(8,128)(2,1)S(1)} %get-tuple-element.162), channel_id=1, source_target_pairs={{0,8},{4,12},{8,0},{12,4},{16,24},{20,28},{24,16},{28,20},{1,9},{5... | collective-permute-start | bytes 3538952 | tf_op jit(solution)/shard_map/ppermute | solution.py:770
  574.5 64.8 %collective-permute-start.43 = (bf16[2,4,24,3072]{3,2,1,0:T(8,128)(2,1)S(1)}, bf16[2,4,24,3072]{3,2,1,0:T(8,128)(2,1)S(1)}, u32[]{:S(2)}, u32[]{:S(2)}) collective-permute-start(bf16[2,4,24,3072]{3,2,1,0:T(8,128)(2,1)S(1)} %get-tuple-element.154), channel_id=1, source_target_pairs={{0,16},{4,20},{8,24},{12,28},{16,0},{20,4},{24,8},{28,12},{1,17},{... | collective-permute-start | bytes 3538952 | tf_op jit(solution)/shard_map/ppermute | solution.py:770
  588.7 53.6 %collective-permute-start.41 = (bf16[2,4,24,3072]{3,2,1,0:T(8,128)(2,1)S(1)}, bf16[2,4,24,3072]{3,2,1,0:T(8,128)(2,1)S(1)}, u32[]{:S(2)}, u32[]{:S(2)}) collective-permute-start(bf16[2,4,24,3072]{3,2,1,0:T(8,128)(2,1)S(1)} %get-tuple-element.166), channel_id=1, source_target_pairs={{0,8},{4,12},{8,0},{12,4},{16,24},{20,28},{24,16},{28,20},{1,9},{5... | collective-permute-start | bytes 3538952 | tf_op jit(solution)/shard_map/ppermute | solution.py:770
  591.8 63.2 %collective-permute-start.28 = (bf16[4,24,3072]{2,1,0:T(8,128)(2,1)S(1)}, bf16[4,24,3072]{2,1,0:T(8,128)(2,1)S(1)}, u32[]{:S(2)}, u32[]{:S(2)}) collective-permute-start(bf16[4,24,3072]{2,1,0:T(8,128)(2,1)S(1)} %fusion.28), channel_id=1, source_target_pairs={{0,8},{4,12},{8,0},{12,4},{16,24},{20,28},{24,16},{28,20},{1,9},{5... | collective-permute-start | bytes 1769480 | tf_op jit(solution)/shard_map/ppermute | solution.py:770
  614.0 41.2 %collective-permute-start.26 = (bf16[4,24,3072]{2,1,0:T(8,128)(2,1)S(1)}, bf16[4,24,3072]{2,1,0:T(8,128)(2,1)S(1)}, u32[]{:S(2)}, u32[]{:S(2)}) collective-permute-start(bf16[4,24,3072]{2,1,0:T(8,128)(2,1)S(1)} %fusion.26), channel_id=1, source_target_pairs={{0,16},{4,20},{8,24},{12,28},{16,0},{20,4},{24,8},{28,12},{1,17},{... | collective-permute-start | bytes 1769480 | tf_op jit(solution)/shard_map/ppermute | solution.py:770
  617.0 50.6 %collective-permute-start.36 = (bf16[4,24,3072]{2,1,0:T(8,128)(2,1)S(1)}, bf16[4,24,3072]{2,1,0:T(8,128)(2,1)S(1)}, u32[]{:S(2)}, u32[]{:S(2)}) collective-permute-start(bf16[4,24,3072]{2,1,0:T(8,128)(2,1)S(1)} %fusion.32), channel_id=1, source_target_pairs={{0,8},{4,12},{8,0},{12,4},{16,24},{20,28},{24,16},{28,20},{1,9},{5... | collective-permute-start | bytes 1769480 | tf_op jit(solution)/shard_map/ppermute | solution.py:770
  639.3 29.5 %collective-permute-start.34 = (bf16[4,24,3072]{2,1,0:T(8,128)(2,1)S(1)}, bf16[4,24,3072]{2,1,0:T(8,128)(2,1)S(1)}, u32[]{:S(2)}, u32[]{:S(2)}) collective-permute-start(bf16[4,24,3072]{2,1,0:T(8,128)(2,1)S(1)} %fusion.30), channel_id=1, source_target_pairs={{0,16},{4,20},{8,24},{12,28},{16,0},{20,4},{24,8},{28,12},{1,17},{... | collective-permute-start | bytes 1769480 | tf_op jit(solution)/shard_map/ppermute | solution.py:770
  642.3 31.8 %collective-permute-start.44 = (bf16[4,24,3072]{2,1,0:T(8,128)(2,1)S(1)}, bf16[4,24,3072]{2,1,0:T(8,128)(2,1)S(1)}, u32[]{:S(2)}, u32[]{:S(2)}) collective-permute-start(bf16[4,24,3072]{2,1,0:T(8,128)(2,1)S(1)} %fusion.36), channel_id=1, source_target_pairs={{0,8},{4,12},{8,0},{12,4},{16,24},{20,28},{24,16},{28,20},{1,9},{5... | collective-permute-start | bytes 1769480 | tf_op jit(solution)/shard_map/ppermute | solution.py:770
  655.0 21.5 %collective-permute-start.42 = (bf16[4,24,3072]{2,1,0:T(8,128)(2,1)S(1)}, bf16[4,24,3072]{2,1,0:T(8,128)(2,1)S(1)}, u32[]{:S(2)}, u32[]{:S(2)}) collective-permute-start(bf16[4,24,3072]{2,1,0:T(8,128)(2,1)S(1)} %fusion.34), channel_id=1, source_target_pairs={{0,16},{4,20},{8,24},{12,28},{16,0},{20,4},{24,8},{28,12},{1,17},{... | collective-permute-start | bytes 1769480 | tf_op jit(solution)/shard_map/ppermute | solution.py:770
  655.6 21.4 %collective-permute-start.29 = (bf16[2,24,3072]{2,1,0:T(8,128)(2,1)S(1)}, bf16[2,24,3072]{2,1,0:T(8,128)(2,1)S(1)}, u32[]{:S(2)}, u32[]{:S(2)}) collective-permute-start(bf16[2,24,3072]{2,1,0:T(8,128)(2,1)S(1)} %get-tuple-element.183), channel_id=1, source_target_pairs={{0,1},{1,2},{2,3},{3,0},{4,5},{5,6},{6,7},{7,4},{8,9},{9,10},{10,1... | collective-permute-start | bytes 884744 | tf_op jit(solution)/shard_map/ppermute | solution.py:811
  667.6 27.4 %collective-permute-start.30 = (bf16[2,24,3072]{2,1,0:T(8,128)(2,1)S(1)}, bf16[2,24,3072]{2,1,0:T(8,128)(2,1)S(1)}, u32[]{:S(2)}, u32[]{:S(2)}) collective-permute-start(bf16[2,24,3072]{2,1,0:T(8,128)(2,1)S(1)} %get-tuple-element.184), channel_id=1, source_target_pairs={{0,2},{1,3},{2,0},{3,1},{4,6},{5,7},{6,4},{7,5},{8,10},{9,11},{10,... | collective-permute-start | bytes 884744 | tf_op jit(solution)/shard_map/ppermute | solution.py:811
  668.8 26.2 %collective-permute-start.31 = (bf16[2,24,3072]{2,1,0:T(8,128)(2,1)S(1)}, bf16[2,24,3072]{2,1,0:T(8,128)(2,1)S(1)}, u32[]{:S(2)}, u32[]{:S(2)}) collective-permute-start(bf16[2,24,3072]{2,1,0:T(8,128)(2,1)S(1)} %get-tuple-element.185), channel_id=1, source_target_pairs={{0,3},{1,0},{2,1},{3,2},{4,7},{5,4},{6,5},{7,6},{8,11},{9,8},{10,9... | collective-permute-start | bytes 884744 | tf_op jit(solution)/shard_map/ppermute | solution.py:811
  674.1 34.7 %collective-permute-start.37 = (bf16[2,24,3072]{2,1,0:T(8,128)(2,1)S(1)}, bf16[2,24,3072]{2,1,0:T(8,128)(2,1)S(1)}, u32[]{:S(2)}, u32[]{:S(2)}) collective-permute-start(bf16[2,24,3072]{2,1,0:T(8,128)(2,1)S(1)} %get-tuple-element.186), channel_id=1, source_target_pairs={{0,1},{1,2},{2,3},{3,0},{4,5},{5,6},{6,7},{7,4},{8,9},{9,10},{10,1... | collective-permute-start | bytes 884744 | tf_op jit(solution)/shard_map/ppermute | solution.py:811
  676.5 42.0 %collective-permute-start.38 = (bf16[2,24,3072]{2,1,0:T(8,128)(2,1)S(1)}, bf16[2,24,3072]{2,1,0:T(8,128)(2,1)S(1)}, u32[]{:S(2)}, u32[]{:S(2)}) collective-permute-start(bf16[2,24,3072]{2,1,0:T(8,128)(2,1)S(1)} %get-tuple-element.187), channel_id=1, source_target_pairs={{0,2},{1,3},{2,0},{3,1},{4,6},{5,7},{6,4},{7,5},{8,10},{9,11},{10,... | collective-permute-start | bytes 884744 | tf_op jit(solution)/shard_map/ppermute | solution.py:811
  676.9 41.6 %collective-permute-start.39 = (bf16[2,24,3072]{2,1,0:T(8,128)(2,1)S(1)}, bf16[2,24,3072]{2,1,0:T(8,128)(2,1)S(1)}, u32[]{:S(2)}, u32[]{:S(2)}) collective-permute-start(bf16[2,24,3072]{2,1,0:T(8,128)(2,1)S(1)} %get-tuple-element.188), channel_id=1, source_target_pairs={{0,3},{1,0},{2,1},{3,2},{4,7},{5,4},{6,5},{7,6},{8,11},{9,8},{10,9... | collective-permute-start | bytes 884744 | tf_op jit(solution)/shard_map/ppermute | solution.py:811
  695.0 23.7 %collective-permute-start.45 = (bf16[2,24,3072]{2,1,0:T(8,128)(2,1)S(1)}, bf16[2,24,3072]{2,1,0:T(8,128)(2,1)S(1)}, u32[]{:S(2)}, u32[]{:S(2)}) collective-permute-start(bf16[2,24,3072]{2,1,0:T(8,128)(2,1)S(1)} %get-tuple-element.189), channel_id=1, source_target_pairs={{0,1},{1,2},{2,3},{3,0},{4,5},{5,6},{6,7},{7,4},{8,9},{9,10},{10,1... | collective-permute-start | bytes 884744 | tf_op jit(solution)/shard_map/ppermute | solution.py:811
  695.0 33.5 %collective-permute-start.46 = (bf16[2,24,3072]{2,1,0:T(8,128)(2,1)S(1)}, bf16[2,24,3072]{2,1,0:T(8,128)(2,1)S(1)}, u32[]{:S(2)}, u32[]{:S(2)}) collective-permute-start(bf16[2,24,3072]{2,1,0:T(8,128)(2,1)S(1)} %get-tuple-element.190), channel_id=1, source_target_pairs={{0,2},{1,3},{2,0},{3,1},{4,6},{5,7},{6,4},{7,5},{8,10},{9,11},{10,... | collective-permute-start | bytes 884744 | tf_op jit(solution)/shard_map/ppermute | solution.py:811
  708.8 19.7 %collective-permute-start.47 = (bf16[2,24,3072]{2,1,0:T(8,128)(2,1)S(1)}, bf16[2,24,3072]{2,1,0:T(8,128)(2,1)S(1)}, u32[]{:S(2)}, u32[]{:S(2)}) collective-permute-start(bf16[2,24,3072]{2,1,0:T(8,128)(2,1)S(1)} %get-tuple-element.191), channel_id=1, source_target_pairs={{0,3},{1,0},{2,1},{3,2},{4,7},{5,4},{6,5},{7,6},{8,11},{9,8},{10,9... | collective-permute-start | bytes 884744 | tf_op jit(solution)/shard_map/ppermute | solution.py:811
  (32 other events, 367.7 us)
Sparse Core Ops, SparseCore 0:
  332.9 144.6 all-reduce.4
